TPU v7x, 32 devices: a whole 2x2x4 slice. The times are simulated.
32 devices in a mesh: lead: 4 (over y, x), lat: 8 (over z, core).
Axes of the slice: x: 2, y: 2, z: 4, core: 2. Of those that a mesh axis runs over, the one named last changes fastest.
Arguments:
- state: float32 [4, 2, 144, 192, 256], P('lead', None, 'lat'), may hold values from -6 to 6
- earlier: float32 [4, 2, 144, 192, 256], P('lead', None, 'lat'), may hold values from -6 to 6
- cotangent: float32 [4, 2, 144, 192, 256], P('lead', None, 'lat'), may hold values from -6 to 6
- level_mask: int32 [4, 2, 144, 192], P('lead', None, 'lat'), may hold values from 0 to 1, as said below
- window_offsets: int32 [4, 2], P('lead'), may hold values from 1 to 11, as said below
- lead_index: int32 [4], P('lead'), may hold values from 0 to 15
- embeddings: float32 [16, 256], replicated, may hold values from -6 to 6
- w_mod: float32 [256, 512], replicated, may hold values from -0.1875 to 0.1875
- b_mod: float32 [512], replicated, may hold values from -4 to 4
- w_qkv: bfloat16 [256, 768], replicated, may hold values from -0.375 to 0.375
- bias_table: float32 [8, 759], replicated, may hold values from -6 to 6
- w_out: bfloat16 [256, 256], replicated, may hold values from -1 to 1
- b_out: float32 [256], replicated, may hold values from -4 to 4
- norm_gain: float32 [256], replicated, may hold values from 0.25 to 1.75
- norm_bias: float32 [256], replicated, may hold values from -4 to 4
- w_up: bfloat16 [256, 1024], replicated, may hold values from -0.375 to 0.375
- b_up: float32 [1024], replicated, may hold values from -6 to 6
- w_down: bfloat16 [1024, 256], replicated, may hold values from -0.375 to 0.375
- b_down: float32 [256], replicated, may hold values from -4 to 4
Outputs:
- block_out: float32 [4, 2, 144, 192, 256], P('lead', None, 'lat')
- state_grad: float32 [4, 2, 144, 192, 256], P('lead', None, 'lat')
- grad_w_mod: float32 [256, 512], replicated
- grad_b_mod: float32 [512], replicated
- grad_w_qkv: float32 [256, 768], replicated
- grad_bias_table: float32 [8, 759], replicated
- grad_w_out: float32 [256, 256], replicated
- grad_b_out: float32 [256], replicated
- grad_norm_gain: float32 [256], replicated
- grad_norm_bias: float32 [256], replicated
- grad_w_up: float32 [256, 1024], replicated
- grad_b_up: float32 [1024], replicated
- grad_w_down: float32 [1024, 256], replicated
- grad_b_down: float32 [256], replicated
Inputs may be any that keep to these rules, and one draw needn't show every extreme that they name: `level_mask`: level 0 tokens are always present; a token of another level is present with probability 0.7. `window_offsets`: column 0 holds latitude offsets of 1 to 5, column 1 longitude offsets of 1 to 11; the top end is taken by some lead time.
All inputs are finite; a program needn't handle non-finite values.
Results may differ from a plain program's by a relative error of at most 0.012.
The roundings to bfloat16 on the way count: a program that leaves them out, or rounds other values in their place, can miss the bound.
Values sent between devices are 32-bit elements; how exact they have to be, the bound alone decides.
A program may use at most 384 MiB of HBM per device.

v0:
```python
import jax
import jax.numpy as jnp
import numpy as np
from jax import lax
from jax.sharding import PartitionSpec as P

HEADS = 8
LEVELS = 2
WLAT = 6
WLON = 12


EPS = 1e-06
NEG = -1000000000.0
HIGH = lax.Precision.HIGHEST


def passed_along(value, axis, steps):
    count = lax.axis_size(axis)
    pairs = [(source, (source + steps) % count) for source in range(count)]
    return lax.ppermute(value, axis, pairs)


def relative_index():
    level_ids, row_ids, col_ids = np.meshgrid(
        np.arange(LEVELS), np.arange(WLAT), np.arange(WLON), indexing="ij"
    )
    level_ids = level_ids.reshape(-1)
    row_ids = row_ids.reshape(-1)
    col_ids = col_ids.reshape(-1)
    span_row = 2 * WLAT - 1
    span_col = 2 * WLON - 1
    level_part = (level_ids[:, None] - level_ids[None, :] + LEVELS - 1) * span_row * span_col
    row_part = (row_ids[:, None] - row_ids[None, :] + WLAT - 1) * span_col
    col_part = col_ids[:, None] - col_ids[None, :] + WLON - 1
    return (level_part + row_part + col_part).astype(np.int32)


def window_tokens(grid):
    shape = grid.shape
    rest = shape[3:]
    blocks = grid.reshape((shape[0], shape[1] // WLAT, WLAT, shape[2] // WLON, WLON) + rest)
    order = (1, 3, 0, 2, 4) + tuple(range(5, 5 + len(rest)))
    return blocks.transpose(order).reshape((-1, LEVELS * WLAT * WLON) + rest)


def grid_tokens(windows, lat_rows, lon_cols):
    rest = windows.shape[2:]
    blocks = windows.reshape((lat_rows // WLAT, lon_cols // WLON, LEVELS, WLAT, WLON) + rest)
    order = (2, 0, 3, 1, 4) + tuple(range(5, 5 + len(rest)))
    return blocks.transpose(order).reshape((LEVELS, lat_rows, lon_cols) + rest)


def normalize_stats(tokens):
    mean_val = jnp.mean(tokens, axis=-1, keepdims=True)
    centered = tokens - mean_val
    inv_dev = lax.rsqrt(jnp.mean(centered * centered, axis=-1, keepdims=True) + EPS)
    return (centered * inv_dev, inv_dev)


def norm_back(grad_hat, normed, inv_dev):
    first = jnp.mean(grad_hat, axis=-1, keepdims=True)
    second = jnp.mean(grad_hat * normed, axis=-1, keepdims=True)
    return inv_dev * (grad_hat - first - normed * second)


def roll_back(grid, head, lat_move, lon_move):
    rows = grid.shape[1]
    cols = grid.shape[2]
    margin = head.shape[1]
    extended = jnp.concatenate([head, grid], axis=1)
    shifted = lax.dynamic_slice_in_dim(extended, margin - lat_move, rows, 1)
    doubled = jnp.concatenate([shifted, shifted], axis=2)
    return lax.dynamic_slice_in_dim(doubled, cols - lon_move, cols, 2)


def on_device(
    state,
    earlier,
    cotangent,
    level_mask,
    window_offsets,
    lead_index,
    embeddings,
    w_mod,
    b_mod,
    w_qkv,
    bias_table,
    w_out,
    b_out,
    norm_gain,
    norm_bias,
    w_up,
    b_up,
    w_down,
    b_down,
):
    f32 = jnp.float32
    bf16 = jnp.bfloat16
    width = state.shape[-1]
    head_size = width // HEADS
    rows = state.shape[2]
    cols = state.shape[3]
    margin = WLAT - 1
    grid_cot = cotangent[0]
    grid_live = level_mask[0].astype(f32)
    lat_shift = window_offsets[0, 0]
    lon_shift = window_offsets[0, 1]
    previous = passed_along(state, "lead", 1)
    grid_in = (previous + earlier)[0]
    first_rows = grid_in[:, :margin]
    side = passed_along((first_rows, grid_live[:, :margin], grid_cot[:, :margin]), "lat", -1)

    def roll_in(grid, tail):
        extended = jnp.concatenate([grid, tail], axis=1)
        shifted = lax.dynamic_slice_in_dim(extended, lat_shift, rows, 1)
        doubled = jnp.concatenate([shifted, shifted], axis=2)
        return lax.dynamic_slice_in_dim(doubled, lon_shift, cols, 2)

    tokens = window_tokens(roll_in(grid_in, side[0]))
    live = window_tokens(roll_in(grid_live, side[1])) > 0.5
    grad_out = window_tokens(roll_in(grid_cot, side[2]))
    windows, span = (tokens.shape[0], tokens.shape[1])
    flat = tokens.reshape(-1, width)
    selector = (jnp.arange(embeddings.shape[0], dtype=jnp.int32) == lead_index[0]).astype(f32)
    emb_row = jnp.dot(selector, embeddings, precision=HIGH)
    modulation = jnp.dot(emb_row, w_mod, precision=HIGH) + b_mod
    shift_one = modulation[:width]
    scale_one = modulation[width:]
    normed, inv_one = normalize_stats(flat)
    ln_in = (normed * (1.0 + scale_one) + shift_one).astype(bf16)
    projected = jnp.dot(ln_in, w_qkv, preferred_element_type=f32).astype(bf16)
    projected = projected.reshape(windows, span, 3, HEADS, head_size)
    queries = projected[:, :, 0]
    key_vals = projected[:, :, 1]
    value_vals = projected[:, :, 2]
    table_index = relative_index()
    bias_full = bias_table[:, table_index]
    scale = head_size ** (-0.5)
    raw = jnp.einsum("wqhd,wkhd->whqk", queries, key_vals, preferred_element_type=f32)
    scores = raw * scale + bias_full[None]
    scores = jnp.where(live[:, None, None, :], scores, NEG)
    peak = jnp.max(scores, axis=-1, keepdims=True)
    expo = jnp.exp(scores - peak)
    weights = expo / jnp.sum(expo, axis=-1, keepdims=True)
    weights_low = weights.astype(bf16)
    attended = jnp.einsum("whqk,wkhd->wqhd", weights_low, value_vals, preferred_element_type=f32)
    attended = attended.astype(bf16).reshape(-1, width)
    mid = flat + jnp.dot(attended, w_out, preferred_element_type=f32) + b_out
    normed_two, inv_two = normalize_stats(mid)
    ln_two = (normed_two * norm_gain + norm_bias).astype(bf16)
    hidden = jnp.dot(ln_two, w_up, preferred_element_type=f32) + b_up
    activ, gelu_back = jax.vjp(jax.nn.gelu, hidden)
    activ_low = activ.astype(bf16)
    result = mid + jnp.dot(activ_low, w_down, preferred_element_type=f32) + b_down
    grad_flat = grad_out.reshape(-1, width)
    branch_grad = grad_flat.astype(bf16)
    g_w_down = jnp.dot(activ_low.T, branch_grad, preferred_element_type=f32)
    g_b_down = jnp.sum(branch_grad.astype(f32), axis=0)
    grad_hidden = gelu_back(jnp.dot(branch_grad, w_down.T, preferred_element_type=f32))[0].astype(
        bf16
    )
    g_w_up = jnp.dot(ln_two.T, grad_hidden, preferred_element_type=f32)
    g_b_up = jnp.sum(grad_hidden.astype(f32), axis=0)
    grad_ln_two = jnp.dot(grad_hidden, w_up.T, preferred_element_type=f32)
    g_gain = jnp.sum(grad_ln_two * normed_two, axis=0)
    g_norm_bias = jnp.sum(grad_ln_two, axis=0)
    grad_mid = grad_flat + norm_back(grad_ln_two * norm_gain, normed_two, inv_two)
    attn_grad = grad_mid.astype(bf16)
    g_w_out = jnp.dot(attended.T, attn_grad, preferred_element_type=f32)
    g_b_out = jnp.sum(attn_grad.astype(f32), axis=0)
    grad_att = jnp.dot(attn_grad, w_out.T, preferred_element_type=f32).astype(bf16)
    grad_att = grad_att.reshape(windows, span, HEADS, head_size)
    kept_low = weights.astype(bf16)
    grad_vals = jnp.einsum("whqk,wqhd->wkhd", kept_low, grad_att, preferred_element_type=f32)
    grad_weights = jnp.einsum("wqhd,wkhd->whqk", grad_att, value_vals, preferred_element_type=f32)
    grad_scores = weights * (grad_weights - jnp.sum(grad_weights * weights, axis=-1, keepdims=True))
    g_bias_table = (
        jnp.zeros(bias_table.shape, f32).at[:, table_index].add(jnp.sum(grad_scores, axis=0))
    )
    grad_raw = (grad_scores * scale).astype(bf16)
    grad_queries = jnp.einsum("whqk,wkhd->wqhd", grad_raw, key_vals, preferred_element_type=f32)
    grad_keys = jnp.einsum("whqk,wqhd->wkhd", grad_raw, queries, preferred_element_type=f32)
    grad_proj = (
        jnp.stack([grad_queries, grad_keys, grad_vals], axis=2).reshape(-1, 3 * width).astype(bf16)
    )
    g_w_qkv = jnp.dot(ln_in.T, grad_proj, preferred_element_type=f32)
    grad_ln_in = jnp.dot(grad_proj, w_qkv.T, preferred_element_type=f32)
    g_shift = jnp.sum(grad_ln_in, axis=0)
    g_scale = jnp.sum(grad_ln_in * normed, axis=0)
    grad_tokens = grad_mid + norm_back(grad_ln_in * (1.0 + scale_one), normed, inv_one)
    grad_mod = jnp.concatenate([g_shift, g_scale])
    outer_mod = emb_row[:, None] * grad_mod[None, :]
    totals = lax.psum(
        (
            g_w_qkv,
            g_bias_table,
            g_w_out,
            g_b_out,
            g_gain,
            g_norm_bias,
            g_w_up,
            g_b_up,
            g_w_down,
            g_b_down,
            outer_mod,
            grad_mod,
        ),
        ("lead", "lat"),
    )
    summed = totals[:10]
    g_w_mod = totals[10]
    g_b_mod = totals[11]
    grid_res = grid_tokens(result.reshape(windows, span, width), rows, cols)
    grid_grad = grid_tokens(grad_tokens.reshape(windows, span, width), rows, cols)
    heads_tail = passed_along(
        (grid_res[:, rows - margin :], grid_grad[:, rows - margin :]), "lat", 1
    )
    out_grid = roll_back(grid_res, heads_tail[0], lat_shift, lon_shift)
    in_grad = roll_back(grid_grad, heads_tail[1], lat_shift, lon_shift)
    state_grad = passed_along(in_grad[None], "lead", -1)
    return (out_grid[None], state_grad, g_w_mod, g_b_mod) + tuple(summed)


def solution(mesh):
    placed = (
        P("lead", None, "lat", None, None),
        P("lead", None, "lat", None, None),
        P("lead", None, "lat", None, None),
        P("lead", None, "lat", None),
        P("lead", None),
        P("lead"),
        P(),
        P(),
        P(),
        P(),
        P(),
        P(),
        P(),
        P(),
        P(),
        P(),
        P(),
        P(),
        P(),
    )
    return jax.shard_map(
        on_device,
        mesh=mesh,
        in_specs=placed,
        out_specs=(
            P("lead", None, "lat", None, None),
            P("lead", None, "lat", None, None),
            P(),
            P(),
            P(),
            P(),
            P(),
            P(),
            P(),
            P(),
            P(),
            P(),
            P(),
            P(),
        ),
        check_vma=False,
    )
```

profile of v0, /device:TPU:18, one launch (start us, length us, event | category | flops | bytes accessed | tf_op | source)
XLA Modules:
  0.0 1303.5 jit_solution(2995791917516773214)
XLA Ops:
  16.7 145.0 %collective-permute-done = f32[1,2,18,192,256]{4,3,2,1,0:T(8,128)} collective-permute-done((f32[1,2,18,192,256]{4,3,2,1,0:T(8,128)}, f32[1,2,18,192,256]{4,3,2,1,0:T(8,128)}, u32[]{:S(2)}, u32[]{:S(2)}) %collective-permute-start) | collective-permute-done | bytes 7077920 | tf_op jit(solution)/shard_map/ppermute | solution.py:21
  161.7 6.1 add_bitcast_fusion
  178.2 38.8 %gather_fusion = f32[20736,8]{1,0:T(8,128)} fusion(f32[8,759]{0,1:T(8,128)S(1)} %copy.184, s32[21504]{0:T(1024)S(1)} %pad_clamp_fusion), kind=kCustom, calls=%fused_computation | custom fusion | bytes 1410048 | tf_op jit(solution)/shard_map/gather | solution.py:138
  217.0 11.9 copy.185
  230.9 3.9 fusion.34
  234.8 5.1 fusion.38
  239.9 11.5 copy.190
  251.4 8.0 copy.191
  259.4 9.1 reshape_reshape.14
  268.5 7.2 convert_reduce_fusion.1
  275.8 5.1 fusion.36
  280.9 5.1 fusion.40
  286.0 11.5 copy.169
  297.4 5.5 bitcast_reduce_fusion
  313.0 6.7 multiply_reduce_fusion.6
  329.9 8.2 copy.263
  338.5 8.9 reshape_reshape.12
  347.5 10.4 convolution_convert_fusion
  357.8 13.9 %copy.177 = bf16[6912,768]{0,1:T(8,128)(2,1)} copy(bf16[6912,768]{1,0:T(8,128)(2,1)} %convolution_convert_fusion) | data formatting | bytes 21233664 | tf_op jit(solution)/shard_map/convert_element_type | solution.py:132
  371.7 33.4 %reshape.163 = bf16[48,144,3,8,32]{1,0,4,3,2:T(8,128)(2,1)} reshape(bf16[6912,768]{0,1:T(8,128)(2,1)} %copy.177) | data formatting | bytes 21233664 | tf_op jit(solution)/shard_map/reshape | solution.py:133
  405.0 14.5 %fusion.92 = (bf16[48,144,1,8,32]{1,0,4,3,2:T(8,128)(2,1)}, bf16[48,144,1,8,32]{1,0,4,3,2:T(8,128)(2,1)}, bf16[48,144,1,8,32]{1,0,4,3,2:T(8,128)(2,1)}) fusion(bf16[48,144,3,8,32]{1,0,4,3,2:T(8,128)(2,1)} %reshape.163), kind=kLoop, calls=%fused_computation.147 | loop fusion | bytes 21233664 | tf_op jit(solution)/shard_map/slice | solution.py:135
  419.5 34.0 %fusion.94 = (f32[48,8,144]{2,1,0:T(8,128)S(1)}, f32[48,8,144,144]{2,3,1,0:T(8,128)}) fusion(f32[8,144,144]{1,2,0:T(8,128)S(1)} %bitcast.149, pred[48,144]{1,0:T(8,128)(4,1)S(1)} %reshape.191, bf16[48,144,1,8,32]{1,0,4,3,2:T(8,128)(2,1)} %get-tuple-element.124, bf16[48,144,1,8,32]{1,0,4,3,2:T(8,128)(2,1)} %get-tuple-element.123), kind=kOutput, calls=%fused_computation.149 | convolution fusion | flops 549421184 | bytes 39820032 | tf_op jit(solution)/shard_map/sub | solution.py:144
  453.6 24.6 %convert_bitcast_fusion = bf16[48,144,8,32]{1,3,2,0:T(8,128)(2,1)} fusion(bf16[48,144,1,8,32]{1,0,4,3,2:T(8,128)(2,1)} %get-tuple-element.125, f32[48,8,144,144]{2,3,1,0:T(8,128)} %get-tuple-element.131, f32[48,8,144]{2,1,0:T(8,128)S(1)} %get-tuple-element.130), kind=kOutput, calls=%fused_computation.89 | convolution fusion | flops 527302656 | bytes 39149568 | tf_op jit(solution)/shard_map/whqk,wkhd->wqhd/dot_general | solution.py:147
  478.2 9.3 copy.187
  487.5 12.2 reshape.164
  499.7 6.2 fusion.95
  506.0 4.0 multiply_reduce_fusion.5
  510.0 11.2 fusion.90
  521.2 32.4 %convert_reduce_fusion = (f32[1024]{0:T(1024)}, bf16[6912,1024]{1,0:T(8,128)(2,1)}, bf16[6912,1024]{1,0:T(8,128)(2,1)}) fusion(f32[6912,1024]{1,0:T(8,128)} %fusion.90, f32[1024]{0:T(1024)S(1)} %copy-done.48, bf16[1024,256]{1,0:T(8,128)(2,1)S(1)} %copy-done, f32[6912,256]{1,0:T(8,128)} %reshape_reshape.14), kind=kOutput, calls=%fused_computation.21 | convolution fusion | flops 3802594304 | bytes 64233472 | tf_op jit(solution)/shard_map/dot_general | solution.py:160
  553.6 14.3 %multiply_reduce_fusion.1 = (f32[256]{0:T(256)}, f32[6912]{0:T(1024)S(1)}, f32[6912]{0:T(1024)S(1)}, f32[256]{0:T(256)}, f32[6912,256]{1,0:T(8,128)S(1)}) fusion(f32[6912,256]{1,0:T(8,128)} %copy-done.1, f32[6912]{0:T(1024)S(1)} %add_rsqrt_fusion.1, f32[6912]{0:T(1024)S(1)} %broadcast_multiply_fusion.6, f32[256]{0:T(256)S(1)} %copy-done.30, ...), kind=kOutput, calls=%fused_computation.70 | convolution fusion | flops 3639789568 | bytes 28949504 | tf_op jit(solution)/shard_map/dot_general | solution.py:165
  567.9 7.1 convert_reduce_fusion.2
  580.8 5.9 copy.192
  586.7 12.6 reshape.167
  599.3 24.4 %fusion.53 = bf16[48,144,1,8,32]{1,4,3,0,2:T(8,128)(2,1)} fusion(bf16[48,144,8,32]{1,0,3,2:T(8,128)(2,1)} %reshape.167, f32[48,8,144,144]{2,3,1,0:T(8,128)} %get-tuple-element.131, f32[48,8,144]{2,1,0:T(8,128)S(1)} %get-tuple-element.130), kind=kOutput, calls=%fused_computation.98 | convolution fusion | flops 525533184 | bytes 39149568 | tf_op jit(solution)/shard_map/whqk,wqhd->wkhd/dot_general | solution.py:175
  623.8 26.6 %fusion.43 = f32[48,8,144,144]{2,3,1,0:T(8,128)} fusion(bf16[48,144,1,8,32]{1,0,4,3,2:T(8,128)(2,1)} %get-tuple-element.125, bf16[48,144,8,32]{1,0,3,2:T(8,128)(2,1)} %reshape.167), kind=kOutput, calls=%fused_computation.92 | convolution fusion | flops 509607936 | bytes 38928384 | tf_op jit(solution)/shard_map/wqhd,wkhd->whqk/dot_general | solution.py:176
  650.4 74.6 %fusion.50 = bf16[48,144,1,8,32]{1,4,3,0,2:T(8,128)(2,1)} fusion(f32[48,8,144,144]{2,3,1,0:T(8,128)} %fusion.43, bf16[48,144,1,8,32]{1,0,4,3,2:T(8,128)(2,1)} %get-tuple-element.124, f32[48,8,144,144]{2,3,1,0:T(8,128)} %get-tuple-element.131, f32[48,8,144]{2,1,0:T(8,128)S(1)} %get-tuple-element.130), kind=kOutput, calls=%fused_computation.97 | convolution fusion | flops 565401728 | bytes 71000064 | tf_op jit(solution)/shard_map/whqk,wqhd->wkhd/dot_general | solution.py:183
  725.0 74.7 %fusion.47 = bf16[48,144,1,8,32]{1,4,3,0,2:T(8,128)(2,1)} fusion(f32[48,8,144,144]{2,3,1,0:T(8,128)} %fusion.43, bf16[48,144,1,8,32]{1,0,4,3,2:T(8,128)(2,1)} %get-tuple-element.123, f32[48,8,144,144]{2,3,1,0:T(8,128)} %get-tuple-element.131, f32[48,8,144]{2,1,0:T(8,128)S(1)} %get-tuple-element.130), kind=kOutput, calls=%fused_computation.96 | convolution fusion | flops 565401728 | bytes 71000064 | tf_op jit(solution)/shard_map/whqk,wkhd->wqhd/dot_general | solution.py:182
  799.8 5.9 add_convert_fusion
  805.7 3.8 copy.202
  809.5 7.0 convert_element_type.92
  816.5 12.0 fusion.64
  828.5 11.8 fusion.24
  840.3 8.9 reshape_reshape.13
  849.3 13.7 %copy.188 = f32[2,3,6,16,12,256]{5,0,4,3,2,1:T(2,128)} copy(f32[2,3,6,16,12,256]{5,4,2,0,3,1:T(8,128)} %bitcast.138) | data formatting | bytes 14155776 | tf_op jit(solution)/shard_map/transpose | solution.py:51
  867.0 10.0 maximum_convert_fusion
  877.0 13.0 copy.198
  890.1 32.0 %convert_element_type.90 = bf16[6912,768]{0,1:T(8,128)(2,1)} reshape(bf16[48,144,3,8,32]{1,0,4,3,2:T(8,128)(2,1)} %copy.198) | data formatting | bytes 21233664 | tf_op jit(solution)/shard_map/convert_element_type | solution.py:185
  922.1 15.7 %multiply_reduce_fusion.2 = (f32[256]{0:T(256)S(1)}, f32[6912]{0:T(1024)S(1)}, f32[6912]{0:T(1024)S(1)}, f32[256]{0:T(256)S(1)}, f32[6912,256]{1,0:T(8,128)}) fusion(f32[6912,256]{1,0:T(8,128)} %reshape_reshape.12, f32[6912]{0:T(1024)S(1)} %copy-done.25, f32[6912]{0:T(1024)S(1)} %copy-done.23, f32[256]{0:T(256)S(1)} %copy-done.29, ...), kind=kOutput, calls=%fused_computation.73 | convolution fusion | flops 2733819904 | bytes 25279488 | tf_op jit(solution)/shard_map/dot_general | solution.py:188
  937.8 5.9 fusion.97
  943.7 9.8 multiply_add_fusion
  953.5 8.7 reshape_reshape.15
  962.3 13.7 %copy.199 = f32[2,3,6,16,12,256]{5,0,4,3,2,1:T(2,128)} copy(f32[2,3,6,16,12,256]{5,4,2,0,3,1:T(8,128)} %bitcast.139) | data formatting | bytes 14155776 | tf_op jit(solution)/shard_map/transpose | solution.py:51
  982.4 6.0 fusion.82
  988.4 12.5 fusion.89
  1004.0 12.6 fusion.33
  1016.6 8.8 fusion.37
  1025.4 4.0 copy.264
  1030.8 69.4 %fusion.96 = f32[8,144,144]{1,2,0:T(8,128)S(1)} fusion(f32[48,8,144,144]{2,3,1,0:T(8,128)} %fusion.43, f32[48,8,144,144]{2,3,1,0:T(8,128)} %get-tuple-element.131, f32[48,8,144]{2,1,0:T(8,128)S(1)} %copy-done.51), kind=kOutput, calls=%fused_computation.151 | output fusion | flops 47665296 | bytes 64585728 | tf_op jit(solution)/shard_map/sub | solution.py:177
  1100.3 10.0 copy.212
  1110.2 112.5 %scatter_custom_fusion = f32[8,759]{0,1:T(8,128)S(1)} fusion(s32[20736]{0:T(1024)} %constant.64, f32[20736,8]{1,0:T(8,128)} %bitcast.147, f32[]{:T(128)} %constant.16.clone.1), kind=kCustom, calls=%fused_computation.110 | custom fusion | flops 165888 | bytes 24800 | tf_op jit(solution)/shard_map/scatter-add | solution.py:179
  1222.8 47.7 %all-reduce = (f32[512]{0:T(512)}, f32[8,759]{0,1:T(8,128)S(1)}, f32[256]{0:T(256)}, f32[256]{0:T(256)}, f32[256]{0:T(256)}, /*index=5*/f32[1024]{0:T(1024)}, f32[256]{0:T(256)}) all-reduce(f32[512]{0:T(512)S(1)} %copy-done.34, f32[8,759]{0,1:T(8,128)S(1)} %scatter_custom_fusion, ...), channel_id=1, replica_groups=mesh['lead'=4,'lat'=8] {'lead','lat'}, use_global_device_ids=true, to_apply=%region_14.15 | all-reduce | flops 8632 | bytes 69056 | tf_op jit(solution)/shard_map/psum | solution.py:194
  1271.3 10.0 fusion.39
  1281.2 4.0 copy.265
  1285.3 6.9 copy.273
  (179 shorter events, 61.2 us)
Async XLA Ops:
  7.2 514.0 %copy-start = (bf16[1024,256]{1,0:T(8,128)(2,1)S(1)}, bf16[1024,256]{1,0:T(8,128)(2,1)}, u32[]{:S(2)}) copy-start(bf16[1024,256]{1,0:T(8,128)(2,1)} %param.39) | copy-start | bytes 1572868
  7.2 1278.0 %all-reduce.4.cloned.1.call-start = ((), (), s32[]{:S(2)}) async-start(), calls=%async_computation | async-start | bytes 7340032 | tf_op jit(solution)/shard_map/psum | solution.py:194
  7.2 154.5 %collective-permute-start = (f32[1,2,18,192,256]{4,3,2,1,0:T(8,128)}, f32[1,2,18,192,256]{4,3,2,1,0:T(8,128)}, u32[]{:S(2)}, u32[]{:S(2)}) collective-permute-start(f32[1,2,18,192,256]{4,3,2,1,0:T(8,128)} %param.22), channel_id=1, source_target_pairs={{0,8},{8,16},{16,24},{24,0},{1,9},{9,17},{17,25},{25,1},{2,10},{10... | collective-permute-start | bytes 21233672 | tf_op jit(solution)/shard_map/ppermute | solution.py:21
  9.6 220.6 %collective-permute-start.2 = (f32[2,5,192]{2,0,1:T(2,128)S(1)}, f32[2,5,192]{2,0,1:T(2,128)S(1)}, u32[]{:S(2)}, u32[]{:S(2)}) collective-permute-start(f32[2,5,192]{2,0,1:T(2,128)S(1)} %slice.52), channel_id=1, source_target_pairs={{0,7},{1,0},{2,1},{3,2},{4,3},{5,4},{6,5},{7,6},{8,15},{9,8},{10,9... | collective-permute-start | bytes 23048 | tf_op jit(solution)/shard_map/ppermute | solution.py:21
  12.6 218.3 %collective-permute-start.4 = (f32[2,5,192,256]{3,2,1,0:T(8,128)}, f32[2,5,192,256]{3,2,1,0:T(8,128)S(1)}, u32[]{:S(2)}, u32[]{:S(2)}) collective-permute-start(f32[2,5,192,256]{3,2,1,0:T(8,128)} %slice.56), channel_id=1, source_target_pairs={{0,7},{1,0},{2,1},{3,2},{4,3},{5,4},{6,5},{7,6},{8,15},{9,8},{10,9... | collective-permute-start | bytes 5898248 | tf_op jit(solution)/shard_map/ppermute | solution.py:21
  16.7 155.4 %copy-start.27 = (s32[20736]{0:T(1024)S(1)}, s32[20736]{0:T(1024)}, u32[]{:S(2)}) copy-start(s32[20736]{0:T(1024)} %constant.64) | copy-start | bytes 248836
  16.7 155.5 %copy-start.45 = (s32[1,2]{1,0:T(1,128)S(1)}, s32[1,2]{1,0:T(1,128)}, u32[]{:S(2)}) copy-start(s32[1,2]{1,0:T(1,128)} %param.26) | copy-start | bytes 28
  16.7 161.2 %copy-start.32 = (f32[8,759]{1,0:T(8,128)S(1)}, f32[8,759]{1,0:T(8,128)}, u32[]{:S(2)}) copy-start(f32[8,759]{1,0:T(8,128)} %param.32) | copy-start | bytes 72868
  167.8 2.9 copy-start.4
  172.1 103.6 %collective-permute-start.1 = (f32[2,5,192,256]{3,2,1,0:T(8,128)}, f32[2,5,192,256]{3,2,1,0:T(8,128)}, u32[]{:S(2)}, u32[]{:S(2)}) collective-permute-start(f32[2,5,192,256]{3,2,1,0:T(8,128)} %slice.50), channel_id=1, source_target_pairs={{0,7},{1,0},{2,1},{3,2},{4,3},{5,4},{6,5},{7,6},{8,15},{9,8},{10,9... | collective-permute-start | bytes 5898248 | tf_op jit(solution)/shard_map/ppermute | solution.py:21
  172.2 175.3 %copy-start.28 = (f32[256]{0:T(256)}, f32[256]{0:T(256)S(1)}, u32[]{:S(2)}) copy-start(f32[256]{0:T(256)S(1)} %get-tuple-element.126) | copy-start | bytes 3076
  172.2 175.3 %copy-start.37 = (f32[256]{0:T(256)}, f32[256]{0:T(256)S(1)}, u32[]{:S(2)}) copy-start(f32[256]{0:T(256)S(1)} %get-tuple-element.127) | copy-start | bytes 3076
  309.9 15.0 %copy-start.6 = (f32[3,16,2,6,12]{1,4,3,2,0:T(8,128)}, f32[3,16,2,6,12]{1,4,3,2,0:T(8,128)S(1)}, u32[]{:S(2)}) copy-start(f32[3,16,2,6,12]{1,4,3,2,0:T(8,128)S(1)} %copy.174) | copy-start | bytes 82948
  329.9 8.2 copy-start.8
  338.3 9.2 copy-start.22
  338.5 9.0 copy-start.24
  338.5 9.0 copy-start.21
  405.0 14.5 %copy-start.9 = (f32[144,144,8]{0,1,2:T(8,128)S(1)}, f32[144,144,8]{0,1,2:T(8,128)}, u32[]{:S(2)}) copy-start(f32[144,144,8]{0,1,2:T(8,128)} %copy.185) | copy-start | bytes 1990660
  453.6 271.4 %copy-start.50 = (f32[48,8,144]{2,1,0:T(8,128)}, f32[48,8,144]{2,1,0:T(8,128)S(1)}, u32[]{:S(2)}) copy-start(f32[48,8,144]{2,1,0:T(8,128)S(1)} %get-tuple-element.130) | copy-start | bytes 663556
  487.5 12.2 copy-start.19
  487.5 12.2 copy-start.42
  505.9 4.1 copy-start.1
  505.9 4.1 copy-start.18
  505.9 4.1 copy-start.30
  505.9 4.1 copy-start.35
  505.9 62.0 %copy-start.11 = (f32[6912]{0:T(1024)}, f32[6912]{0:T(1024)S(1)}, u32[]{:S(2)}) copy-start(f32[6912]{0:T(1024)S(1)} %broadcast_multiply_fusion.6) | copy-start | bytes 82948
  510.0 57.9 %copy-start.16 = (f32[6912]{0:T(1024)}, f32[6912]{0:T(1024)S(1)}, u32[]{:S(2)}) copy-start(f32[6912]{0:T(1024)S(1)} %add_rsqrt_fusion.1) | copy-start | bytes 82948
  510.0 11.2 copy-start.48
  553.6 14.3 %copy-start.2 = (f32[6912,256]{1,0:T(8,128)S(1)}, f32[6912,256]{1,0:T(8,128)}, u32[]{:S(2)}) copy-start(f32[6912,256]{1,0:T(8,128)} %copy-done.1) | copy-start | bytes 21233668
  575.0 2.9 copy-start.3
  725.0 74.8 %copy-start.7 = (f32[3,16,2,6,12]{1,4,3,2,0:T(8,128)S(1)}, f32[3,16,2,6,12]{1,4,3,2,0:T(8,128)}, u32[]{:S(2)}) copy-start(f32[3,16,2,6,12]{1,4,3,2,0:T(8,128)} %copy-done.6) | copy-start | bytes 82948
  725.0 74.8 %copy-start.10 = (f32[3,16,2,6,12]{1,4,3,2,0:T(8,128)S(1)}, f32[3,16,2,6,12]{1,4,3,2,0:T(8,128)}, u32[]{:S(2)}) copy-start(f32[3,16,2,6,12]{1,4,3,2,0:T(8,128)} %copy.201) | copy-start | bytes 82948
  725.0 74.8 %copy-start.29 = (f32[256]{0:T(256)S(1)}, f32[256]{0:T(256)}, u32[]{:S(2)}) copy-start(f32[256]{0:T(256)} %copy-done.28) | copy-start | bytes 3076
  725.0 74.8 %copy-start.38 = (f32[256]{0:T(256)S(1)}, f32[256]{0:T(256)}, u32[]{:S(2)}) copy-start(f32[256]{0:T(256)} %copy-done.37) | copy-start | bytes 3076
  809.5 19.0 %slice-start = ((s8[7077888]{0:T(1024)(128)(4,1)}), s8[2883584]{0:T(1024)(128)(4,1)S(1)}, s32[]{:S(2)}) async-start(s8[7077888]{0:T(1024)(128)(4,1)} %bitcast.125), calls=%async_computation.1 | async-start | bytes 5767168
  816.5 12.0 slice-start.1
  816.5 12.0 copy-start.49
  866.5 134.4 %collective-permute-start.3 = (f32[2,5,192,256]{3,0,2,1:T(2,128)}, f32[2,5,192,256]{3,0,2,1:T(2,128)}, u32[]{:S(2)}, u32[]{:S(2)}) collective-permute-start(f32[2,5,192,256]{3,0,2,1:T(2,128)} %slice.55), channel_id=1, source_target_pairs={{0,1},{1,2},{2,3},{3,4},{4,5},{5,6},{6,7},{7,0},{8,9},{9,10},{10,1... | collective-permute-start | bytes 5898248 | tf_op jit(solution)/shard_map/ppermute | solution.py:21
  890.1 32.0 %copy-start.23 = (f32[6912]{0:T(1024)S(1)}, f32[6912]{0:T(1024)}, u32[]{:S(2)}) copy-start(f32[6912]{0:T(1024)} %copy-done.22) | copy-start | bytes 82948
  890.1 32.0 %copy-start.25 = (f32[6912]{0:T(1024)S(1)}, f32[6912]{0:T(1024)}, u32[]{:S(2)}) copy-start(f32[6912]{0:T(1024)} %copy-done.24) | copy-start | bytes 82948
  890.1 53.7 %slice-start.4 = ((s8[7077888]{0:T(1024)(128)(4,1)}), s8[2883584]{0:T(1024)(128)(4,1)S(1)}, s32[]{:S(2)}) async-start(s8[7077888]{0:T(1024)(128)(4,1)} %bitcast.129), calls=%async_computation.5 | async-start | bytes 5767168
  922.1 15.7 %copy-start.5 = (bf16[6912,768]{0,1:T(8,128)(2,1)S(1)}, bf16[6912,768]{0,1:T(8,128)(2,1)}, u32[]{:S(2)}) copy-start(bf16[6912,768]{0,1:T(8,128)(2,1)} %convert_element_type.90) | copy-start | bytes 31850500
  922.1 21.6 %slice-start.5 = ((s8[7077888]{0:T(1024)(128)(4,1)}), s8[4194304]{0:T(1024)(128)(4,1)S(1)}, s32[]{:S(2)}) async-start(s8[7077888]{0:T(1024)(128)(4,1)} %bitcast.129), calls=%async_computation.6 | async-start | bytes 8388608
  962.3 19.2 %copy-start.40 = (f32[1,256]{1,0:T(1,128)S(1)}, f32[1,256]{1,0:T(1,128)}, u32[]{:S(2)}) copy-start(f32[1,256]{1,0:T(1,128)} %copy-done.39) | copy-start | bytes 3076
  976.0 12.4 slice-start.2
  976.0 12.4 copy-start.12
  976.0 12.4 copy-start.17
  976.0 12.4 copy-start.31
  976.0 12.4 copy-start.36
  979.7 24.3 %collective-permute-start.5 = (f32[2,5,192,256]{3,0,2,1:T(2,128)}, f32[2,5,192,256]{3,0,2,1:T(2,128)S(1)}, u32[]{:S(2)}, u32[]{:S(2)}) collective-permute-start(f32[2,5,192,256]{3,0,2,1:T(2,128)} %slice.57), channel_id=1, source_target_pairs={{0,1},{1,2},{2,3},{3,4},{4,5},{5,6},{6,7},{7,0},{8,9},{9,10},{10,1... | collective-permute-start | bytes 5898248 | tf_op jit(solution)/shard_map/ppermute | solution.py:21
  982.4 6.0 slice-start.3
  1025.4 5.4 copy-start.51
  1029.4 255.8 %collective-permute-start.6 = (f32[1,2,18,192,256]{4,3,2,1,0:T(8,128)}, f32[1,2,18,192,256]{4,3,2,1,0:T(8,128)}, u32[]{:S(2)}, u32[]{:S(2)}) collective-permute-start(f32[1,2,18,192,256]{4,3,2,1,0:T(8,128)} %bitcast.122), channel_id=1, source_target_pairs={{0,24},{8,0},{16,8},{24,16},{1,25},{9,1},{17,9},{25,17},{2,26},{10... | collective-permute-start | bytes 21233672 | tf_op jit(solution)/shard_map/ppermute | solution.py:21
  1100.2 122.6 %copy-start.34 = (f32[512]{0:T(512)S(1)}, f32[512]{0:T(512)}, u32[]{:S(2)}) copy-start(f32[512]{0:T(512)} %copy-done.33) | copy-start | bytes 6148
  1100.2 122.6 %copy-start.41 = (f32[1024]{0:T(1024)S(1)}, f32[1024]{0:T(1024)}, u32[]{:S(2)}) copy-start(f32[1024]{0:T(1024)} %get-tuple-element.118) | copy-start | bytes 12292
  1100.2 122.6 %copy-start.43 = (f32[256]{0:T(256)S(1)}, f32[256]{0:T(256)}, u32[]{:S(2)}) copy-start(f32[256]{0:T(256)} %get-tuple-element.120) | copy-start | bytes 3076
  1100.2 122.6 %copy-start.44 = (f32[256]{0:T(256)S(1)}, f32[256]{0:T(256)}, u32[]{:S(2)}) copy-start(f32[256]{0:T(256)} %convert_reduce_fusion.1) | copy-start | bytes 3076
  1100.2 122.6 %copy-start.46 = (f32[256]{0:T(256)S(1)}, f32[256]{0:T(256)}, u32[]{:S(2)}) copy-start(f32[256]{0:T(256)} %get-tuple-element.98) | copy-start | bytes 3076
  1100.2 122.6 %copy-start.47 = (f32[256]{0:T(256)S(1)}, f32[256]{0:T(256)}, u32[]{:S(2)}) copy-start(f32[256]{0:T(256)} %get-tuple-element.104) | copy-start | bytes 3076
  1285.2 6.9 copy-start.20
  1285.2 7.7 copy-start.15
  1285.2 8.6 copy-start.26
  1285.2 9.3 copy-start.14
  1285.2 10.2 copy-start.13
  (2 other events, 2.0 us)
Sparse Core Ops, SparseCore 0:
  1001.1 269.0 all-reduce.3
where the time goes:
time: 1310 us; the launch traced here: 1300 us
  matrix products  403 us (31%)
  local copies, waits for them, and re-layouts  377 us (29%)
  other arithmetic  301 us (23%)
  waiting for transfers between devices  148 us (11%)
  blocking collectives  47.7 us (4%)
  between operations  22.2 us (2%)
    ppermute x7, waiting for transfers between devices, passed_along(): return lax.ppermute(value, axis, pairs)  148 us
    scatter-add x1, other arithmetic, on_device(): jnp.zeros(bias_table.shape, f32).at[:, table_index]  112 us
    dot_general x1, matrix products, on_device(): jnp.einsum('whqk,wkhd->wqhd', grad_raw, key_vals, preferred_element_type=...  74.7 us
    dot_general x1, matrix products, on_device(): jnp.einsum('whqk,wqhd->wkhd', grad_raw, queries, preferred_element_type=f32)  74.6 us
    sub x1, other arithmetic, on_device(): grad_weights - jnp.sum(grad_weights * weights, axis=-1, keepdims=True)  69.4 us
    gather x2, local copies, waits for them, and re-layouts, on_device(): bias_full = bias_table[:, table_index]  50.7 us
    psum x1, blocking collectives, on_device(): lax.psum((g_w_qkv, g_bias_table, g_w_out, g_b_out, g_gain, g_norm_bias, g...  47.7 us
    convert_element_type x2, local copies, waits for them, and re-layouts, on_device(): jnp.stack([grad_queries, grad_keys, grad_vals], axis=2)  45 us
  transfers between devices with their start and end apart: 8, of which 2 were waited for; matrix products, arithmetic and copies ran while one was open for 36% of the time, Pallas kernels for 0%

commit v1 on v0

v1 whole, which is shorter than its diff:
```python
import functools

import jax
import jax.numpy as jnp
import numpy as np
from jax import lax
from jax.experimental import pallas as pl
from jax.experimental.pallas import tpu as pltpu
from jax.sharding import PartitionSpec as P

HEADS = 8
LEVELS = 2
WLAT = 6
WLON = 12
SPAN = LEVELS * WLAT * WLON
MARGIN = WLAT - 1
SPAN_ROW = 2 * WLAT - 1
SPAN_COL = 2 * WLON - 1
TABLE_ROWS = (2 * LEVELS - 1) * SPAN_ROW * SPAN_COL
TABLE_PAD = 768
TILE = 128
REST = SPAN - TILE
LOG2E = 1.4426950408889634
GELU_ONE = 0.7978845608028654
GELU_TWO = GELU_ONE * 0.044715
REACH = 24
BLOCK = 48
WIDE = 512

EPS = 1e-06
NEG = -1000000000.0
HIGH = lax.Precision.HIGHEST
F32 = jnp.float32
BF16 = jnp.bfloat16
VMEM = pltpu.VMEM
WHOLE = pl.BlockSpec(memory_space=pltpu.VMEM)
SMEM = pl.BlockSpec(memory_space=pltpu.SMEM)
ANYWHERE = pl.BlockSpec(memory_space=pl.ANY)
SMALL = pl.CostEstimate(flops=1, bytes_accessed=1, transcendentals=0)
LIMIT = 30 * 1024 * 1024
BLOCK_LIMIT = 48 * 1024 * 1024


def passed_along(value, axis, steps):
    count = lax.axis_size(axis)
    pairs = [(source, (source + steps) % count) for source in range(count)]
    return lax.ppermute(value, axis, pairs)


def in_hbm(array):
    return pltpu.with_memory_space_constraint(array, pltpu.HBM)


def dot_nn(a, b):
    return lax.dot_general(a, b, (((1,), (0,)), ((), ())), preferred_element_type=F32)


def prepare_kernel(count, table_ref, *refs):
    out_ref, scratch = refs[-count - 2], refs[-1]
    for source, target in zip(refs[:count], refs[-count - 1 : -1]):
        target[...] = source[...].T
    table = table_ref[...]
    lanes = lax.broadcasted_iota(jnp.int32, (384, SPAN), 0)
    cell = lax.broadcasted_iota(jnp.int32, (384, SPAN), 1)
    place = (
        (cell // (WLAT * WLON)) * (SPAN_ROW * SPAN_COL)
        + ((cell // WLON) % WLAT) * SPAN_COL
        + cell % WLON
    )
    pick = (lanes == place).astype(F32)
    base = (SPAN_ROW * SPAN_COL) * (LEVELS - 1) + SPAN_COL * (WLAT - 1) + WLON - 1
    for group in range(LEVELS * WLAT):
        level, row = divmod(group, WLAT)
        start = level * SPAN_ROW * SPAN_COL + row * SPAN_COL - group * WLON - base
        moved = pltpu.roll(table, start % TABLE_PAD, 1)
        for head in range(HEADS):
            scratch[head, pl.ds(group * WLON, WLON), :] = jnp.broadcast_to(
                moved[head : head + 1], (WLON, TABLE_PAD)
            )
    for head in range(HEADS):
        rows = pltpu.roll(scratch[head], 0, 1, stride=1, stride_axis=0)
        values = jnp.dot(rows[:, :384], pick, precision=HIGH, preferred_element_type=F32) * LOG2E
        out_ref[:, pl.ds(head * TILE, TILE)] = values[:, :TILE]
        out_ref[:, pl.ds(HEADS * TILE + head * REST, REST)] = values[:, TILE:]


def prepare(bias_table, weights, after):
    padded = jnp.pad(bias_table, ((0, 0), (0, TABLE_PAD - TABLE_ROWS)))
    return pl.pallas_call(
        functools.partial(prepare_kernel, len(weights)),
        out_shape=[jax.ShapeDtypeStruct((SPAN, HEADS * SPAN), F32)]
        + [jax.ShapeDtypeStruct(array.shape[::-1], array.dtype) for array in weights],
        in_specs=[WHOLE] * (1 + len(weights)) + [ANYWHERE] * len(after),
        out_specs=[WHOLE] * (1 + len(weights)),
        scratch_shapes=[VMEM((HEADS, SPAN, TABLE_PAD), F32)],
        compiler_params=pltpu.CompilerParams(vmem_limit_bytes=LIMIT),
        cost_estimate=SMALL,
        name="prepare",
    )(padded, *weights, *after)


def collect_kernel(first, width, leads, lead_ref, grad_ref, small_ref, *refs):
    out_ref, extra, sem = refs[-3:]
    cell = lax.broadcasted_iota(jnp.int32, (SPAN, TABLE_PAD), 0)
    lanes = lax.broadcasted_iota(jnp.int32, (SPAN, TABLE_PAD), 1)
    place = (
        (cell // (WLAT * WLON)) * (SPAN_ROW * SPAN_COL)
        + ((cell // WLON) % WLAT) * SPAN_COL
        + cell % WLON
    )
    base = (SPAN_ROW * SPAN_COL) * (LEVELS - 1) + SPAN_COL * (WLAT - 1) + WLON - 1
    spread = (lanes == base - place).astype(F32)
    extra[...] = jnp.zeros_like(extra)
    count = small_ref.shape[1] // width
    sums = jnp.sum(small_ref[...], axis=0, keepdims=True)
    for index in range(count):
        extra[pl.ds(index, 1), :] = sums[:, index * width : (index + 1) * width]
    at = count
    for head in range(HEADS):
        parts = [
            grad_ref[:, pl.ds(head * TILE, TILE)],
            grad_ref[:, pl.ds(HEADS * TILE + head * REST, REST)],
        ]
        wide = jnp.dot(
            jnp.concatenate(parts, axis=1), spread, precision=HIGH, preferred_element_type=F32
        )
        wide = pltpu.roll(wide, 0, 1, stride=1, stride_axis=0)
        total = None
        for group in range(LEVELS * WLAT):
            level, row = divmod(group, WLAT)
            start = level * SPAN_ROW * SPAN_COL + row * SPAN_COL - group * WLON
            part = jnp.sum(wide[group * WLON : (group + 1) * WLON], axis=0, keepdims=True)
            part = pltpu.roll(jnp.broadcast_to(part, (8, TABLE_PAD)), start % TABLE_PAD, 1)
            total = part if total is None else total + part
        for index in range(TABLE_PAD // width):
            extra[pl.ds(at, 1), :] = total[0:1, index * width : (index + 1) * width]
            at += 1
    for index in range(2):
        value = sums[:, (4 + index) * width : (5 + index) * width]
        extra[pl.ds(at + leads * index + lead_ref[0], 1), :] = value
    copy = pltpu.make_async_copy(extra, out_ref.at[pl.ds(first, extra.shape[0]), :], sem)
    copy.start()
    copy.wait()


def collect(lead_index, leads, bias, small, buffer, first, after):
    rows, width = buffer.shape
    return pl.pallas_call(
        functools.partial(collect_kernel, first, width, leads),
        out_shape=jax.ShapeDtypeStruct(buffer.shape, F32),
        in_specs=[SMEM, WHOLE, WHOLE, ANYWHERE] + [ANYWHERE] * len(after),
        out_specs=ANYWHERE,
        scratch_shapes=[VMEM((rows - first, width), F32), pltpu.SemaphoreType.DMA],
        input_output_aliases={3: 0},
        compiler_params=pltpu.CompilerParams(vmem_limit_bytes=LIMIT),
        cost_estimate=SMALL,
        name="collect",
    )(lead_index, bias, small, buffer, *after)


class Peers:
    def __init__(self, lats, leads, rows, send_sems, got_sems):
        self.lead = lax.axis_index("lead")
        lat = lax.axis_index("lat")
        self.core = lax.rem(lat, 2)
        self.chip = lax.div(lat, 2)
        self.chips, self.leads = lats // 2, leads
        self.half = rows // 2
        self.part = self.half // self.chips
        self.piece = self.part // leads
        self.pair = (self.lead, lat + 1 - 2 * self.core)
        self.along_lat = [
            (self.lead, 2 * lax.rem(self.chip + d, self.chips) + self.core)
            for d in range(1, self.chips)
        ]
        self.along_lead = [(lax.rem(self.lead + d, leads), lat) for d in range(1, leads)]
        self.sems = (send_sems, got_sems)
        self.count = 0

    def meet(self, peers):
        barrier = pltpu.get_barrier_semaphore()
        for peer in peers:
            pl.semaphore_signal(
                barrier, inc=1, device_id=peer, device_id_type=pl.DeviceIdType.MESH
            )
        pl.semaphore_wait(barrier, len(peers))

    def send(self, source, target, peer):
        copy = pltpu.make_async_remote_copy(
            src_ref=source,
            dst_ref=target,
            send_sem=self.sems[0].at[self.count],
            recv_sem=self.sems[1].at[self.count],
            device_id=peer,
            device_id_type=pl.DeviceIdType.MESH,
        )
        self.count += 1
        copy.start()
        return copy


def some_rows(start, size):
    return pl.ds(pl.multiple_of(start, 8), size)


def scatter_kernel(lats, leads, in_ref, *refs):
    out_ref, got_pair, sum_pair, got_lat, sum_lat, got_lead, send_sems, got_sems = refs[-8:]
    at = Peers(lats, leads, in_ref.shape[0], send_sems, got_sems)
    at.meet([at.pair] + at.along_lat + at.along_lead)
    at.send(in_ref.at[some_rows((1 - at.core) * at.half, at.half), :], got_pair, at.pair).wait()
    sum_pair[...] = in_ref[some_rows(at.core * at.half, at.half), :] + got_pair[...]
    copies = [
        at.send(
            sum_pair.at[some_rows(lax.rem(at.chip + d, at.chips) * at.part, at.part), :],
            got_lat.at[d - 1],
            at.along_lat[d - 1],
        )
        for d in range(1, at.chips)
    ]
    for copy in copies:
        copy.wait()
    total = sum_pair[some_rows(at.chip * at.part, at.part), :]
    for d in range(1, at.chips):
        total = total + got_lat[d - 1]
    sum_lat[...] = total
    copies = [
        at.send(
            sum_lat.at[some_rows(lax.rem(at.lead + d, leads) * at.piece, at.piece), :],
            got_lead.at[d - 1],
            at.along_lead[d - 1],
        )
        for d in range(1, leads)
    ]
    for copy in copies:
        copy.wait()
    mine = some_rows(at.lead * at.piece, at.piece)
    total = sum_lat[mine, :]
    for d in range(1, leads):
        total = total + got_lead[d - 1]
    out_ref[mine, :] = total
    copies = [at.send(out_ref.at[mine, :], out_ref.at[mine, :], peer) for peer in at.along_lead]
    for copy in copies:
        copy.wait()


def scattered_sum(buffer, after):
    rows, width = buffer.shape
    lats = lax.axis_size("lat")
    leads = lax.axis_size("lead")
    chips = lats // 2
    half = rows // 2
    part = half // chips
    piece = part // leads
    copies = chips + 2 * leads - 2
    return pl.pallas_call(
        functools.partial(scatter_kernel, lats, leads),
        out_shape=jax.ShapeDtypeStruct((part, width), F32),
        in_specs=[WHOLE] + [ANYWHERE] * len(after),
        out_specs=WHOLE,
        scratch_shapes=[
            VMEM((half, width), F32),
            VMEM((half, width), F32),
            VMEM((chips - 1, part, width), F32),
            VMEM((part, width), F32),
            VMEM((leads - 1, piece, width), F32),
            pltpu.SemaphoreType.DMA((copies,)),
            pltpu.SemaphoreType.DMA((copies,)),
        ],
        compiler_params=pltpu.CompilerParams(
            vmem_limit_bytes=LIMIT, collective_id=0, has_side_effects=True
        ),
        cost_estimate=SMALL,
        name="scattered_sum",
    )(buffer, *after)


def hold_kernel(count, *refs):
    for source, target in zip(refs[:count], refs[-count:]):
        target[...] = source[...]


def held_until(arrays, after):
    return pl.pallas_call(
        functools.partial(hold_kernel, len(arrays)),
        out_shape=[jax.ShapeDtypeStruct(array.shape, F32) for array in arrays],
        in_specs=[WHOLE] * len(arrays) + [ANYWHERE] * len(after),
        out_specs=[WHOLE] * len(arrays),
        compiler_params=pltpu.CompilerParams(vmem_limit_bytes=LIMIT),
        cost_estimate=SMALL,
        name="hold",
    )(*arrays, *after)


def gathered(part, after):
    lats = lax.axis_size("lat")
    far = [passed_along(part, "lat", 2 * d) for d in range(1, lats // 2)]
    own = [part] + list(held_until(far, after))
    pairs = [(source, source ^ 1) for source in range(lats)]
    return own, [lax.ppermute(array, "lat", pairs) for array in own]


def finish_kernel(chips, hidden, embed_rows, place_ref, embed_ref, *refs):
    parts, others = refs[:chips], refs[chips : 2 * chips]
    outs, buffer = refs[2 * chips : -1], refs[-1]
    part, width = parts[0].shape
    core, chip = place_ref[0], place_ref[1]
    for index in range(chips):
        at = lax.rem(chip + chips - index, chips) * part
        buffer[some_rows(core * (chips * part) + at, part), :] = parts[index][...]
        buffer[some_rows((1 - core) * (chips * part) + at, part), :] = others[index][...]
    g_mod, g_b_mod, g_qkv, g_table, g_out, g_b_out, g_gain, g_bias, g_up, g_b_up, g_down, g_b_down = outs
    for index in range(3):
        lanes = slice(index * width, (index + 1) * width)
        g_qkv[:, lanes] = buffer[index * width : (index + 1) * width, :]
    g_out[...] = buffer[3 * width : 4 * width, :]
    for index in range(hidden // width):
        lanes = slice(index * width, (index + 1) * width)
        at = 4 * width + index * width
        g_up[:, lanes] = buffer[at : at + width, :]
        at += hidden
        g_down[lanes, :] = buffer[at : at + width, :].T
    at = 4 * width + 2 * hidden
    for place, (target, index) in enumerate(
        [(g_b_down, 0), (g_gain, 0), (g_bias, 0), (g_b_out, 0), (g_b_mod, 0), (g_b_mod, 1)]
        + [(g_b_up, index) for index in range(hidden // width)]
    ):
        target[:, index * width : (index + 1) * width] = buffer[at + place : at + place + 1, :]
    at += 6 + hidden // width
    each = TABLE_PAD // width
    heads = []
    for head in range(HEADS):
        first = at + head * each
        heads.append(
            jnp.concatenate([buffer[first + i : first + i + 1, :] for i in range(each)], axis=1)
        )
    before = lax.broadcasted_iota(jnp.int32, (TABLE_PAD, TABLE_PAD), 0)
    behind = lax.broadcasted_iota(jnp.int32, (TABLE_PAD, TABLE_PAD), 1)
    turn = (before + behind == TABLE_ROWS - 1).astype(F32)
    turned = jnp.dot(
        jnp.concatenate(heads, axis=0), turn, precision=HIGH, preferred_element_type=F32
    )
    g_table[...] = turned[:, :TABLE_ROWS]
    at += HEADS * each
    for index in range(2):
        lanes = slice(index * width, (index + 1) * width)
        rows = buffer[at + index * embed_rows : at + (index + 1) * embed_rows, :]
        g_mod[:, lanes] = jnp.dot(
            embed_ref[...], rows, precision=HIGH, preferred_element_type=F32
        )


def finished(own, others, embeddings, width, hidden):
    chips = len(own)
    lat = lax.axis_index("lat")
    place = jnp.stack([lat % 2, lat // 2]).astype(jnp.int32)
    shapes = [(width, 2 * width), (1, 2 * width), (width, 3 * width), (HEADS, TABLE_ROWS)]
    shapes += [(width, width), (1, width), (1, width), (1, width), (width, hidden), (1, hidden)]
    shapes += [(hidden, width), (1, width)]
    outs = pl.pallas_call(
        functools.partial(finish_kernel, chips, hidden, embeddings.shape[0]),
        out_shape=[jax.ShapeDtypeStruct(shape, F32) for shape in shapes],
        in_specs=[SMEM] + [WHOLE] * (1 + 2 * chips),
        out_specs=[WHOLE] * len(shapes),
        scratch_shapes=[VMEM((2 * chips * own[0].shape[0], width), F32)],
        compiler_params=pltpu.CompilerParams(vmem_limit_bytes=LIMIT),
        cost_estimate=SMALL,
        name="finish",
    )(place, embeddings.T, *own, *others)
    return tuple(out.reshape(-1) if out.shape[0] == 1 else out for out in outs)


def roll_kernel(specs, rows, *refs):
    offsets, own = refs[0], refs[1]
    sems = refs[-1]
    grids = refs[-1 - len(specs) : -1]
    outs = refs[-1 - 2 * len(specs) : -1 - len(specs)]
    copies = []
    for spec, grid in zip(specs, grids):
        started = []
        for place, first, width, halo, halo_first in spec["pieces"]:
            for half in range(2):
                lanes = pl.ds(128 * half, 128)
                cols = pl.ds(place, width)
                for source, begin, target in (
                    (own, first, grid.at[:, pl.ds(0, rows), half, cols, :]),
                    (refs[2 + halo], halo_first, grid.at[:, pl.ds(rows, MARGIN), half, cols, :]),
                ):
                    copy = pltpu.make_async_copy(
                        source.at[:, :, pl.ds(begin, width), lanes],
                        target,
                        sems.at[sum(map(len, copies)) + len(started)],
                    )
                    copy.start()
                    started.append(copy)
        copies.append(started)
    lat_shift = offsets[0]
    lon_shift = offsets[1]
    for spec, grid, out_ref, started in zip(specs, grids, outs, copies):
        for copy in started:
            copy.wait()
        for column in range(spec["count"]):
            start = spec["start"] + column * WLON + lon_shift
            for step in range(rows // WLAT):
                for level in range(LEVELS):
                    for row in range(WLAT):
                        token = step * SPAN + (level * WLAT + row) * WLON
                        for half in range(2):
                            lanes = slice(128 * half, 128 * half + 128)
                            out_ref[column, pl.ds(token, WLON), lanes] = grid[
                                level,
                                lat_shift + step * WLAT + row,
                                half,
                                pl.ds(start, WLON),
                                :,
                            ]


def roll_in(offsets, grid, halos, parts, after):
    rows, cols, features = grid.shape[1:]
    used, specs, scratch, out_shape = [], [], [], []
    for begin, end in parts:
        low = (begin * WLON + 1) // 8 * 8
        high = (end * WLON + WLON - 2) // 8 * 8 + 8
        pieces = []
        for wrap in range(2):
            for first, array in halos:
                left = max(low - wrap * cols, first)
                right = min(high - wrap * cols, first + array.shape[2])
                if left < right:
                    place = left + wrap * cols - low
                    pieces.append((place, left, right - left, len(used), left - first))
                    used.append(array)
        specs.append(dict(pieces=pieces, start=begin * WLON - low, count=end - begin))
        scratch.append(VMEM((LEVELS, rows + MARGIN, 2, high - low, 128), F32))
        shape = (end - begin, rows // WLAT * SPAN, features)
        out_shape.append(jax.ShapeDtypeStruct(shape, F32))
    count = 4 * sum(len(spec["pieces"]) for spec in specs)
    return pl.pallas_call(
        functools.partial(roll_kernel, specs, rows),
        out_shape=out_shape,
        in_specs=[SMEM] + [ANYWHERE] * (1 + len(used) + len(after)),
        out_specs=[WHOLE] * len(parts),
        scratch_shapes=scratch + [pltpu.SemaphoreType.DMA((count,))],
        compiler_params=pltpu.CompilerParams(vmem_limit_bytes=LIMIT),
        cost_estimate=SMALL,
        name="roll_in",
    )(offsets, in_hbm(grid), *used, *after)


def margin_kernel(near, low, cols, first_ref, second_ref, *refs):
    near_ref, far_ref, sems = refs[-3:]
    copies = []
    for index, source in enumerate((first_ref, second_ref)):
        for begin, width, target, place in (
            (0, near, near_ref, 0),
            (low, cols - low, far_ref, 0),
            (0, 16, far_ref, cols - low),
        ):
            copy = pltpu.make_async_copy(
                source.at[:, pl.ds(0, MARGIN), pl.ds(begin, width), :],
                target.at[index, :, :, pl.ds(place, width), :],
                sems.at[len(copies)],
            )
            copy.start()
            copies.append(copy)
    for copy in copies:
        copy.wait()


def margins_of(first, second, near, low, after):
    levels, _, cols, features = first.shape
    return pl.pallas_call(
        functools.partial(margin_kernel, near, low, cols),
        out_shape=[
            jax.ShapeDtypeStruct((2, levels, MARGIN, near, features), F32),
            jax.ShapeDtypeStruct((2, levels, MARGIN, cols - low + 16, features), F32),
        ],
        in_specs=[ANYWHERE] * (2 + len(after)),
        out_specs=[WHOLE] * 2,
        scratch_shapes=[pltpu.SemaphoreType.DMA((6,))],
        compiler_params=pltpu.CompilerParams(vmem_limit_bytes=LIMIT),
        cost_estimate=SMALL,
        name="margins",
    )(in_hbm(first), in_hbm(second), *after)


def unroll_kernel(spec, rows, *refs):
    offsets = refs[0]
    count = spec["count"]
    own = refs[1 : 1 + count]
    tail = refs[1 + count : 1 + 2 * count]
    if spec["targets"]:
        out_hbm, grid, out_ref, sems = refs[-4:]
    else:
        out_ref, grid = refs[-2:]
    lat_shift = offsets[0]
    lon_shift = offsets[1]
    for column in range(count):
        for level in range(LEVELS):
            for row in range(WLAT):
                token = (level * WLAT + row) * WLON
                for half in range(2):
                    lanes = slice(128 * half, 128 * half + 128)
                    cols = pl.ds(column * WLON, WLON)
                    grid[level, row, half, cols, :] = tail[column][0, pl.ds(token, WLON), lanes]
                    for step in range(rows // WLAT):
                        grid[level, WLAT + step * WLAT + row, half, cols, :] = own[column][
                            0, pl.ds(step * SPAN + token, WLON), lanes
                        ]
    start = spec["start"] - lon_shift
    width = spec["width"]
    copies = []
    for level in range(LEVELS):
        for row in range(rows):
            for half in range(2):
                out_ref[level, row, :, 128 * half : 128 * half + 128] = grid[
                    level, WLAT + row - lat_shift, half, pl.ds(start, width), :
                ]
        for place, first, size in spec["targets"]:
            copy = pltpu.make_async_copy(
                out_ref.at[level, :, pl.ds(place, size), :],
                out_hbm.at[level, :, pl.ds(first, size), :],
                sems.at[len(copies)],
            )
            copy.start()
            copies.append(copy)
    for copy in copies:
        copy.wait()


def targets_of(start, end, cols):
    edge = min(end, cols)
    return [(0, start, edge - start)] + ([(cols - start, 0, end - cols)] if end > cols else [])


def roll_back(offsets, own, tail, first, start, end, shape, after, into=()):
    count = len(own)
    levels, rows, cols, features = shape
    tokens = own[0][0].shape[1]
    width = end - start
    spec = dict(count=count, start=start - first, width=width)
    spec["targets"] = targets_of(start, end, cols) if into else []

    def spec_of(entry, tall):
        index, lane = (entry[1:] + (0,))[:2]
        return pl.BlockSpec((1, tall, features), lambda i: (index, 0, lane))

    scratch = [VMEM((levels, rows + WLAT, 2, count * WLON + 16, 128), F32)]
    piece = (levels, rows, width, features)
    base = [array for array in into if array is not None]
    if into:
        out_shape, out_spec = shape, ANYWHERE
        scratch += [VMEM(piece, F32), pltpu.SemaphoreType.DMA((2 * levels,))]
    else:
        out_shape, out_spec = piece, pl.BlockSpec(piece, lambda i: (0, 0, 0, 0))
    return pl.pallas_call(
        functools.partial(unroll_kernel, spec, rows),
        out_shape=(pltpu.HBM if into else jax.ShapeDtypeStruct)(out_shape, F32),
        grid=(1,),
        in_specs=[SMEM]
        + [spec_of(entry, tokens) for entry in own]
        + [spec_of(entry, SPAN) for entry in tail]
        + [ANYWHERE] * (len(base) + len(after)),
        out_specs=out_spec,
        scratch_shapes=scratch,
        input_output_aliases={1 + 2 * count: 0} if base else {},
        compiler_params=pltpu.CompilerParams(vmem_limit_bytes=LIMIT),
        cost_estimate=SMALL,
        name="roll_back",
    )(
        offsets,
        *[in_hbm(entry[0]) for entry in own],
        *[entry[0] for entry in tail],
        *[in_hbm(array) for array in base],
        *after,
    )


def place_kernel(targets, piece_hbm, *refs):
    out_hbm, held, sems = refs[-3:]
    inward, outward = [], []
    for level in range(LEVELS):
        copy = pltpu.make_async_copy(piece_hbm.at[level], held.at[level], sems.at[level])
        copy.start()
        inward.append(copy)
    for level in range(LEVELS):
        inward[level].wait()
        for place, first, size in targets:
            copy = pltpu.make_async_copy(
                held.at[level, :, pl.ds(place, size), :],
                out_hbm.at[level, :, pl.ds(first, size), :],
                sems.at[LEVELS + len(outward)],
            )
            copy.start()
            outward.append(copy)
    for copy in outward:
        copy.wait()


def placed_in(grid, piece, start, shape, after):
    targets = targets_of(start, start + piece.shape[2], shape[2])
    base = [] if grid is None else [grid]
    return pl.pallas_call(
        functools.partial(place_kernel, targets),
        out_shape=pltpu.HBM(shape, F32),
        in_specs=[ANYWHERE] * (1 + len(base) + len(after)),
        out_specs=ANYWHERE,
        scratch_shapes=[VMEM(piece.shape, F32), pltpu.SemaphoreType.DMA((3 * LEVELS,))],
        input_output_aliases={1: 0} if base else {},
        compiler_params=pltpu.CompilerParams(vmem_limit_bytes=LIMIT),
        cost_estimate=SMALL,
        name="place",
    )(piece, *[in_hbm(array) for array in base], *after)


def row_sums(value):
    return jnp.sum(value.reshape(value.shape[0] // 8, 8, value.shape[1]), axis=0)


def block_kernel(
    begin,
    halo_first,
    given,
    waits,
    offsets,
    recv_ref,
    earlier_hbm,
    cot_hbm,
    halo_hbm,
    live_ref,
    mod_ref,
    w_qkv_ref,
    w_qkv_t_ref,
    bias_ref,
    w_out_ref,
    w_out_t_ref,
    vec_ref,
    w_up_ref,
    w_up_t_ref,
    b_up_ref,
    w_down_ref,
    w_down_t_ref,
    *refs,
):
    (
        res_ref,
        grad_ref,
        tail_ref,
        acc_main,
        acc_bias,
        acc_small,
        fetched,
        sems,
        x_s,
        g_s,
        normed_s,
        inv_s,
        ln_in_s,
        proj_s,
        prob_s,
        prob_low_s,
        q_wide_s,
        d_wide_s,
        dscore_s,
        q_wide_t,
        d_wide_t,
        att_t,
        dq_t,
        ln_two_s,
        act_s,
        dhid_s,
        branch_s,
        attg_s,
        gproj_s,
        att_s,
        gatt_s,
        normed_two_s,
        inv_two_s,
        first_s,
        pre_s,
        back_s,
        turned_one,
        turned_two,
    ) = refs[given + waits :]
    width = recv_ref.shape[-1]
    tokens = recv_ref.shape[1]
    count = tokens // SPAN
    hidden = w_up_ref.shape[1]
    head_size = width // HEADS
    wide = HEADS * SPAN
    scale = head_size ** (-0.5)

    @pl.when(pl.program_id(0) == 0)
    def _():
        for index, target in enumerate((acc_main, acc_bias, acc_small)):
            target[...] = refs[index][...] if given else jnp.zeros_like(target)

    step = pl.program_id(0)
    grid_rows = earlier_hbm.shape[1]
    grid_cols = earlier_hbm.shape[2]
    lat_shift = offsets[0]
    lon_shift = offsets[1]

    def place_of(at):
        first = (begin + at) * WLON + lon_shift
        return first // 8 * 8, first % 8

    def copies_of(at, slot):
        first, _ = place_of(at)
        whole, split = [], []
        for index, source in enumerate((earlier_hbm, cot_hbm)):
            for half in range(2):
                lanes = pl.ds(128 * half, 128)
                own = fetched.at[slot, index, :, pl.ds(0, grid_rows), half]
                sem = sems.at[slot, 4 * index + 2 * half]
                cols = pl.ds(pl.multiple_of(first, 8), REACH)
                whole.append((source.at[:, :, cols, lanes], own, sem))
                for j in range(0, REACH, 8):
                    cols = pl.ds(pl.multiple_of((first + j) % grid_cols, 8), 8)
                    split.append((source.at[:, :, cols, lanes], own.at[:, :, pl.ds(j, 8), :], sem))
        return whole, split

    def halo_copies_of(at, slot):
        first, _ = place_of(at)
        cols = pl.ds(pl.multiple_of(first - halo_first, 8), REACH)
        copies = []
        for index in range(2):
            for half in range(2):
                copies.append(
                    (
                        halo_hbm.at[index, :, :, cols, pl.ds(128 * half, 128)],
                        fetched.at[slot, index, :, pl.ds(grid_rows, MARGIN), half],
                        sems.at[slot, 4 * index + 2 * half + 1],
                    )
                )
        return copies

    def fetch(at, slot):
        first, _ = place_of(at)
        whole, split = copies_of(at, slot)

        @pl.when(first + REACH <= grid_cols)
        def _():
            for copy in whole:
                pltpu.make_async_copy(*copy).start()

        @pl.when(first + REACH > grid_cols)
        def _():
            for copy in split:
                pltpu.make_async_copy(*copy).start()

        for copy in halo_copies_of(at, slot):
            pltpu.make_async_copy(*copy).start()

    slot = step % 2

    @pl.when(step == 0)
    def _():
        fetch(0, 0)

    @pl.when(step + 1 < pl.num_programs(0))
    def _():
        fetch(step + 1, 1 - slot)

    for source, target, sem in copies_of(0, slot)[0] + halo_copies_of(0, slot):
        pltpu.make_async_copy(source, target, sem).wait()
    _, inside = place_of(step)
    for index, target in enumerate((x_s, g_s)):
        for part in range(count):
            for level in range(LEVELS):
                for row in range(WLAT):
                    token = part * SPAN + (level * WLAT + row) * WLON
                    for half in range(2):
                        target[pl.ds(token, WLON), 128 * half : 128 * half + 128] = fetched[
                            slot, index, level, lat_shift + part * WLAT + row, half, pl.ds(inside, WLON), :
                        ]

    shift_one = mod_ref[0:1, :]
    gain_one = mod_ref[1:2, :]
    b_out = vec_ref[0:1, :]
    gain_two = vec_ref[1:2, :]
    bias_two = vec_ref[2:3, :]
    b_down = vec_ref[3:4, :]

    group = 128 // head_size
    groups = [
        (slice(first * TILE, (first + group) * TILE), slice(first * head_size, first * head_size + 128))
        for first in range(0, HEADS, group)
    ]
    rest = slice(HEADS * TILE, wide)

    @pl.when(step == 0)
    def _():
        for part in range(count):
            for lanes, own in groups + [(rest, slice(0, width))]:
                for target in (q_wide_s, d_wide_s):
                    target[part, lanes, own] = jnp.zeros_like(target[part, lanes, own])
                for target in (q_wide_t, d_wide_t):
                    target[part, own, lanes] = jnp.zeros_like(target[part, own, lanes])

    def spread_heads(value, turned, target, target_t):
        for head in range(HEADS):
            own = slice(head * head_size, (head + 1) * head_size)
            tile = pl.ds(head * TILE, TILE)
            rest = pl.ds(HEADS * TILE + head * REST, REST)
            target[tile, own] = value[:TILE, own]
            target[rest, own] = value[TILE:, own]
            target_t[own, tile] = turned[own, :TILE]
            target_t[own, rest] = turned[own, TILE:]

    def head_products(turned, scores, target):
        last = dot_nn(turned, scores[:, pl.ds(HEADS * TILE, HEADS * REST)])
        for head in range(HEADS):
            own = slice(head * head_size, (head + 1) * head_size)
            first = dot_nn(turned[own, :], scores[:, pl.ds(head * TILE, TILE)])
            target[own, 0:TILE] = first.astype(BF16)
            target[own, TILE:SPAN] = last[own, head * REST : (head + 1) * REST].astype(BF16)

    def wide_product(left, wide_t, start, size):
        features = slice(0, width)
        if start < rest.start:
            features = groups[start // (group * TILE)][1]
        return dot_nn(left[:, features], wide_t[features, start : start + size])

    def wide_sum(scores, wide_s):
        parts = [dot_nn(scores[:, lanes], wide_s[lanes, own]) for lanes, own in groups]
        return jnp.concatenate(parts, axis=1) + dot_nn(scores[:, rest], wide_s[rest, :])

    everything = count * SPAN
    blocks = [slice(start, start + BLOCK) for start in range(0, everything, BLOCK)]
    items = [
        (part, start, min(WIDE, wide - start))
        for part in range(count)
        for start in range(0, wide, WIDE)
    ]

    def rows_of(part):
        return slice(part * SPAN, (part + 1) * SPAN)

    def ahead(products, work):
        held = products[0]()
        for index in range(len(products)):
            later = products[index + 1]() if index + 1 < len(products) else None
            work(index, held)
            held = later

    def normalized(value):
        centered = value - jnp.mean(value, axis=-1, keepdims=True)
        inv = lax.rsqrt(jnp.mean(centered * centered, axis=-1, keepdims=True) + EPS)
        return centered * inv, inv

    def norm_back(hat, normed, inv):
        first = jnp.mean(hat, axis=-1, keepdims=True)
        second = jnp.mean(hat * normed, axis=-1, keepdims=True)
        return inv * (hat - first - normed * second)

    def add_small(place, values):
        acc_small[:, place * width : (place + 1) * width] += functools.reduce(jnp.add, values)

    for rows in blocks:
        x = recv_ref[0, rows, :] + x_s[rows, :]
        x_s[rows, :] = x
        normed, inv = normalized(x)
        normed_s[rows, :] = normed
        inv_s[rows, :] = inv
        ln_in_s[rows, :] = (normed * gain_one + shift_one).astype(BF16)
    for start in range(0, 3 * width, WIDE):
        lanes = slice(start, min(start + WIDE, 3 * width))
        proj_s[:, lanes] = dot_nn(ln_in_s[...], w_qkv_ref[:, lanes]).astype(BF16)

    live = []
    for part in range(count):
        rows = rows_of(part)
        live.append(jnp.broadcast_to(live_ref[0, rows, :], (SPAN, 128)))
        queries = proj_s[rows, 0:width]
        spread_heads(queries, queries.T, q_wide_s.at[part], q_wide_t.at[part])

    def raw_scores(item):
        part, start, size = item
        keys = proj_s[rows_of(part), width : 2 * width]
        return wide_product(keys, q_wide_t.at[part], start, size)

    def softmax(index, raw):
        part, start, size = items[index]
        for place in range(0, size, 128):
            lanes = slice(start + place, start + place + 128)
            scores = raw[:, place : place + 128] * (scale * LOG2E) + bias_ref[:, lanes]
            scores = jnp.where(live[part] > 0.5, scores, NEG)
            expo = jnp.exp2(scores - jnp.max(scores, axis=0, keepdims=True))
            prob = expo * (1.0 / jnp.sum(expo, axis=0, keepdims=True))
            prob_s[part, :, lanes] = prob
            prob_low_s[part, :, lanes] = prob.astype(BF16)
        if start + size == wide:
            values_t = proj_s[rows_of(part), 2 * width : 3 * width].T
            head_products(values_t, prob_low_s.at[part], att_t.at[part])

    ahead([functools.partial(raw_scores, item) for item in items], softmax)

    for part in range(count):
        att_s[rows_of(part), :] = att_t[part].T
    first_s[...] = dot_nn(att_s[...], w_out_ref[...])
    for rows in blocks:
        mid = x_s[rows, :] + first_s[rows, :] + b_out
        x_s[rows, :] = mid
        normed, inv = normalized(mid)
        normed_two_s[rows, :] = normed
        inv_two_s[rows, :] = inv
        ln_two_s[rows, :] = (normed * gain_two + bias_two).astype(BF16)
        branch_s[rows, :] = g_s[rows, :].astype(BF16)

    def feed(start):
        lanes = slice(start, start + WIDE)
        slot = start // WIDE % 2
        pre_s[slot] = dot_nn(ln_two_s[...], w_up_ref[:, lanes])
        back_s[slot] = dot_nn(branch_s[...], w_down_t_ref[:, lanes])

    def gelu(index, _):
        for first in range(0, WIDE, width):
            gelu_part(index * WIDE + first, index % 2, slice(first, first + width))

    def gelu_part(start, slot, inside):
        lanes = slice(start, start + width)
        sums = []
        for rows in blocks:
            pre = pre_s[slot, rows, inside] + b_up_ref[:, lanes]
            square = pre * pre
            half = 0.5 + 0.5 * jnp.tanh(pre * (GELU_ONE + GELU_TWO * square))
            act_s[rows, lanes] = (pre * half).astype(BF16)
            slope = pre * (2 * GELU_ONE + (6 * GELU_TWO) * square)
            dhid = back_s[slot, rows, inside] * (half * (1.0 + (1.0 - half) * slope))
            dhid = dhid.astype(BF16)
            dhid_s[rows, lanes] = dhid
            sums.append(row_sums(dhid.astype(F32)))
        add_small(6 + start // width, sums)

    ahead([functools.partial(feed, start) for start in range(0, hidden, WIDE)], gelu)

    first_s[...] = dot_nn(dhid_s[...], w_up_t_ref[...])
    res_ref[0] = dot_nn(act_s[...], w_down_ref[...])
    sums = [[], [], [], []]
    for rows in blocks:
        g_ln = first_s[rows, :]
        normed = normed_two_s[rows, :]
        grad_mid = g_s[rows, :] + norm_back(g_ln * gain_two, normed, inv_two_s[rows, :])
        grad_ref[0, rows, :] = grad_mid
        att_grad = grad_mid.astype(BF16)
        attg_s[rows, :] = att_grad
        for place, value in enumerate(
            (branch_s[rows, :].astype(F32), g_ln * normed, g_ln, att_grad.astype(F32))
        ):
            sums[place].append(row_sums(value))
    for place in range(4):
        add_small(place, sums[place])

    gatt_s[...] = dot_nn(attg_s[...], w_out_t_ref[...]).astype(BF16)
    for rows in blocks:
        result = res_ref[0, rows, :] + x_s[rows, :] + b_down
        res_ref[0, rows, :] = result
        if rows.start >= (count - 1) * SPAN:
            start = rows.start - (count - 1) * SPAN
            tail_ref[0, start : start + BLOCK, 0:width] = result
    for part in range(count):
        g_att = gatt_s[rows_of(part), :]
        spread_heads(g_att, g_att.T, d_wide_s.at[part], d_wide_t.at[part])

    def add_main(place, total):
        acc_main[place * width : (place + 1) * width, :] += total

    def out_gradient():
        total = dot_nn(att_t[0], attg_s[rows_of(0), :])
        for part in range(1, count):
            total += dot_nn(att_t[part], attg_s[rows_of(part), :])
        add_main(3, total)

    def feed_gradient(place, left, right, start):
        total = dot_nn(left[...], right[:, start : start + WIDE])
        for first in range(0, total.shape[1], width):
            add_main(place + first // width, total[:, first : first + width])

    turned_one[...] = ln_two_s[...].T
    turned_two[...] = branch_s[...].T
    extra = [out_gradient]
    for start in range(0, hidden, WIDE):
        place = 4 + start // width
        extra.append(functools.partial(feed_gradient, place, turned_one, dhid_s, start))
    for start in range(0, hidden, WIDE):
        place = 4 + (hidden + start) // width
        extra.append(functools.partial(feed_gradient, place, turned_two, act_s, start))

    def d_probs(item):
        part, start, size = item
        values = proj_s[rows_of(part), 2 * width : 3 * width]
        return wide_product(values, d_wide_t.at[part], start, size)

    def d_scores(index, d_prob):
        part, start, size = items[index]
        rows = rows_of(part)
        if extra:
            extra.pop(0)()
        for place in range(0, size, 128):
            lanes = slice(start + place, start + place + 128)
            own = d_prob[:, place : place + 128]
            prob = prob_s[part, :, lanes]
            inside = jnp.sum(own * prob, axis=0, keepdims=True)
            d_score = prob * (own - inside)
            acc_bias[:, lanes] += d_score
            dscore_s[part, :, lanes] = (d_score * scale).astype(BF16)
        if start + size == wide:
            d_values = wide_sum(prob_low_s.at[part], d_wide_s.at[part])
            d_keys = wide_sum(dscore_s.at[part], q_wide_s.at[part])
            keys_t = proj_s[rows, width : 2 * width].T
            head_products(keys_t, dscore_s.at[part], dq_t.at[part])
            gproj_s[rows, 0:width] = dq_t[part].T
            gproj_s[rows, width : 2 * width] = d_keys.astype(BF16)
            gproj_s[rows, 2 * width : 3 * width] = d_values.astype(BF16)

    ahead([functools.partial(d_probs, item) for item in items], d_scores)
    for rest in extra:
        rest()

    first_s[...] = dot_nn(gproj_s[...], w_qkv_t_ref[...])
    turned_one[...] = ln_in_s[...].T
    for start in range(0, 3 * width, WIDE):
        feed_gradient(start // width, turned_one, gproj_s, start)
    sums = [[], []]
    for rows in blocks:
        g_ln = first_s[rows, :]
        normed = normed_s[rows, :]
        total = grad_ref[0, rows, :] + norm_back(g_ln * gain_one, normed, inv_s[rows, :])
        grad_ref[0, rows, :] = total
        if rows.start >= (count - 1) * SPAN:
            start = rows.start - (count - 1) * SPAN
            tail_ref[0, start : start + BLOCK, width : 2 * width] = total
        sums[0].append(row_sums(g_ln))
        sums[1].append(row_sums(g_ln * normed))
    for place in range(2):
        add_small(4 + place, sums[place])


def run_block(
    offsets, begin, received, earlier, cot, halo, halo_first, live, fixed, sums, sum_shapes, after
):
    columns, tall, width = received.shape
    count = tall // SPAN
    hidden = fixed[7].shape[1]
    wide = HEADS * SPAN
    rows = earlier.shape[1]

    def moving(tall_size, last, first=0):
        return pl.BlockSpec((1, tall_size, last), lambda i: (i + first, 0, 0))

    def still(array):
        place = (0,) * len(array.shape)
        return pl.BlockSpec(array.shape, lambda i: place, pipeline_mode=pl.Buffered(1))

    in_specs = [SMEM, moving(tall, width)] + [ANYWHERE] * 3 + [moving(tall, 1, begin)]
    first_sum = len(in_specs) + len(fixed)
    in_specs += [still(array) for array in fixed] + [still(array) for array in sums]
    in_specs += [ANYWHERE] * len(after)
    shapes = [pltpu.HBM(sum_shapes[0], F32)]
    shapes += [jax.ShapeDtypeStruct(shape, F32) for shape in sum_shapes[1:]]
    out_specs = [moving(tall, width)] * 2 + [moving(SPAN, 2 * width)] + [still(a) for a in shapes]
    out_shape = (
        [pltpu.HBM((columns, tall, width), F32)] * 2
        + [jax.ShapeDtypeStruct((columns, SPAN, 2 * width), F32)]
        + shapes
    )
    return pl.pallas_call(
        functools.partial(block_kernel, begin, halo_first, len(sums), len(after)),
        out_shape=out_shape,
        grid=(columns,),
        in_specs=in_specs,
        out_specs=out_specs,
        scratch_shapes=[
            VMEM((2, 2, LEVELS, rows + MARGIN, 2, 24, 128), F32),
            pltpu.SemaphoreType.DMA((2, 8)),
            VMEM((tall, width), F32),
            VMEM((tall, width), F32),
            VMEM((tall, width), F32),
            VMEM((tall, 1), F32),
            VMEM((tall, width), BF16),
            VMEM((tall, 3 * width), BF16),
            VMEM((count, SPAN, wide), F32),
            VMEM((count, SPAN, wide), BF16),
            VMEM((count, wide, width), BF16),
            VMEM((count, wide, width), BF16),
            VMEM((count, SPAN, wide), BF16),
            VMEM((count, width, wide), BF16),
            VMEM((count, width, wide), BF16),
            VMEM((count, width, SPAN), BF16),
            VMEM((count, width, SPAN), BF16),
            VMEM((tall, width), BF16),
            VMEM((tall, hidden), BF16),
            VMEM((tall, hidden), BF16),
            VMEM((tall, width), BF16),
            VMEM((tall, width), BF16),
            VMEM((tall, 3 * width), BF16),
            VMEM((tall, width), BF16),
            VMEM((tall, width), BF16),
            VMEM((tall, width), F32),
            VMEM((tall, 1), F32),
            VMEM((tall, width), F32),
            VMEM((2, tall, WIDE), F32),
            VMEM((2, tall, WIDE), F32),
            VMEM((width, tall), BF16),
            VMEM((width, tall), BF16),
        ],
        input_output_aliases={first_sum + i: 3 + i for i in range(len(sums))},
        compiler_params=pltpu.CompilerParams(vmem_limit_bytes=BLOCK_LIMIT),
        cost_estimate=pl.CostEstimate(
            flops=columns * 10**10, bytes_accessed=1, transcendentals=0
        ),
        name="block",
    )(offsets, received, in_hbm(earlier), in_hbm(cot), halo, live, *fixed, *sums, *after)


def window_tokens(grid):
    shape = grid.shape
    blocks = grid.reshape((shape[0], shape[1] // WLAT, WLAT, shape[2] // WLON, WLON))
    return blocks.transpose((3, 1, 0, 2, 4)).reshape((shape[2] // WLON, -1, 1))


SHARES = (4, 4, 4, 4)


def on_device(
    state,
    earlier,
    cotangent,
    level_mask,
    window_offsets,
    lead_index,
    embeddings,
    w_mod,
    b_mod,
    w_qkv,
    bias_table,
    w_out,
    b_out,
    norm_gain,
    norm_bias,
    w_up,
    b_up,
    w_down,
    b_down,
):
    width = state.shape[-1]
    rows = state.shape[2]
    cols = state.shape[3]
    hidden = w_up.shape[1]
    total = cols // WLON
    offsets = window_offsets[0]
    lat_shift = offsets[0]
    lon_shift = offsets[1]
    ends = [int(total * share) // sum(SHARES) for share in np.cumsum(SHARES)]
    steps = list(zip([0] + ends[:-1], ends))
    near = ((ends[0] - 1) * WLON + WLON - 1) // 8 * 8 + REACH
    far = (ends[0] * WLON + 1) // 8 * 8

    next_offsets = passed_along(offsets, "lead", -1)
    state_halos = [
        (low, passed_along(state[0][:, :MARGIN, low:high], "lat", -1))
        for low, high in ((0, near), (near, cols))
    ]
    grid_live = level_mask[0].astype(F32)
    live_halo = passed_along(grid_live[:, :MARGIN], "lat", -1)
    moved = []
    for step in steps:
        moved += roll_in(next_offsets, state[0], state_halos, [step], moved[-1:] or [live_halo])
    received = [passed_along(array, "lead", 1) for array in moved]
    margins = margins_of(earlier[0], cotangent[0], near, far, moved[:1])
    halos = [passed_along(margin, "lat", -1) for margin in margins]

    extended = jnp.concatenate([grid_live, live_halo], axis=1)
    shifted = lax.dynamic_slice_in_dim(extended, lat_shift, rows, 1)
    doubled = jnp.concatenate([shifted, shifted], axis=2)
    live = window_tokens(lax.dynamic_slice_in_dim(doubled, lon_shift, cols, 2))

    emb_row = lax.dynamic_index_in_dim(embeddings, lead_index[0], 0, keepdims=False)
    modulation = jnp.dot(emb_row, w_mod, precision=HIGH) + b_mod
    mod = jnp.stack([modulation[:width], 1.0 + modulation[width:]])
    vectors = jnp.stack([b_out, norm_gain, norm_bias, b_down])
    bias, w_qkv_t, w_out_t, w_up_t, w_down_t = prepare(
        bias_table, [w_qkv, w_out, w_up, w_down], moved[1:2]
    )
    fixed = [
        mod,
        w_qkv,
        w_qkv_t,
        bias,
        w_out,
        w_out_t,
        vectors,
        w_up,
        w_up_t,
        b_up[None],
        w_down,
        w_down_t,
    ]
    main_rows = 4 * width + 2 * hidden
    few = 6 * width + hidden
    table_rows = HEADS * TABLE_PAD // width
    mod_rows = 2 * embeddings.shape[0]
    used = main_rows + few // width + table_rows + mod_rows
    unit = 8 * lax.axis_size("lat") * lax.axis_size("lead")
    buffer_rows = -(-used // unit) * unit
    sum_shapes = [(buffer_rows, width), (SPAN, HEADS * SPAN), (8, few)]
    sums = []

    results, grads = [], []
    shape = earlier.shape[1:]

    def back(kept, start, end, after, into=()):
        low = (start - (WLON - 1)) // WLON
        high = (end - 2) // WLON
        picked = [kept[window % total] for window in range(low, high + 1)]
        own, tail = zip(*picked)
        return roll_back(offsets, own, tail, low * WLON, start, end, shape, after, into)

    bounds = [(end * WLON + 1) // 16 * 16 for end in ends[:-1]] + [cols + 16]
    pieces = list(zip([16] + bounds[:-1], bounds))
    rolled, grad_pieces = [], []
    for index, (begin, end) in enumerate(steps):
        made = run_block(
            offsets,
            begin,
            received[index],
            earlier[0],
            cotangent[0],
            halos[min(index, 1)],
            0 if index == 0 else far,
            live,
            fixed,
            sums,
            sum_shapes,
            moved[1:2] if index == 0 else rolled[-1:],
        )
        sums = made[3:]
        tail = passed_along(made[2], "lat", 1)
        for window in range(begin, end):
            results.append(((made[0], window - begin), (tail, window - begin, 0)))
            grads.append(((made[1], window - begin), (tail, window - begin, 1)))
        if index == len(steps) - 2:
            rolled.append(back(grads, pieces[0][0], pieces[index - 1][1], [made[4]]))
            grad_pieces.append(passed_along(rolled[-1], "lead", -1))
    rolled.append(back(grads, *pieces[-2], [made[4]]))
    grad_pieces.append(passed_along(rolled[-1], "lead", -1))
    buffer = collect(lead_index, embeddings.shape[0], sums[1], sums[2], sums[0], main_rows, rolled[-1:])
    part = scattered_sum(buffer, [])
    rolled.append(back(grads, *pieces[-1], [part] + grad_pieces))
    grad_pieces.append(passed_along(rolled[-1], "lead", -1))
    block_out = back(results, pieces[0][0], pieces[-3][1], rolled[-1:], (None,))
    block_out = back(results, pieces[-2][0], pieces[-1][1], [], (block_out,))
    state_grad = placed_in(None, grad_pieces[0], pieces[0][0], shape, [in_hbm(block_out)])
    state_grad = placed_in(state_grad, grad_pieces[1], pieces[-2][0], shape, [])
    own, others = gathered(part, [in_hbm(state_grad)])
    state_grad = placed_in(state_grad, grad_pieces[2], pieces[-1][0], shape, [])
    outs = finished(own, others, embeddings, width, hidden)
    return (block_out[None], state_grad[None]) + outs


def solution(mesh):
    grid = P("lead", None, "lat", None, None)
    placed = (grid, grid, grid, P("lead", None, "lat", None), P("lead", None), P("lead"))
    return jax.shard_map(
        on_device,
        mesh=mesh,
        in_specs=placed + (P(),) * 13,
        out_specs=(grid, grid) + (P(),) * 12,
        check_vma=False,
    )
```

time: 1310 us -> 361 us (0.28)
  matrix products: 403 us -> 1.06 us
  local copies, waits for them, and re-layouts: 377 us -> 12.5 us
  other arithmetic: 301 us -> 1.02 us
  Pallas kernels: 0 us -> 270 us
  waiting for transfers between devices: 148 us -> 41.9 us
  blocking collectives: 47.7 us -> 0 us
  starting transfers between devices: 5.3 us -> 22.3 us
  between operations: 22.2 us -> 6.02 us
    dot_general x18 -> x0, matrix products: 367 us -> none  [the longest x1 74.7 us: on_device(): jnp.einsum('whqk,wkhd->wqhd', grad_raw, key_vals, preferred_element_type=...]
    pallas_call x0 -> x22, Pallas kernels: none -> 270 us  [the longest x4 148 us: run_block(): pl.pallas_call(functools.partial(block_kernel, begin, halo_first, len(sum...]
    scatter-add x1 -> x0, other arithmetic: 112 us -> none  [on_device(): jnp.zeros(bias_table.shape, f32).at[:, table_index]]
    ppermute x7 -> x20, waiting for transfers between devices: 148 us -> 39.3 us  [passed_along(): return lax.ppermute(value, axis, pairs)]
    convert_element_type x7 -> x0, local copies, waits for them, and re-layouts: 84.8 us -> none  [the longest x2 45 us: on_device(): jnp.stack([grad_queries, grad_keys, grad_vals], axis=2)]
    sub x1 -> x0, other arithmetic: 69.4 us -> none  [on_device(): grad_weights - jnp.sum(grad_weights * weights, axis=-1, keepdims=True)]
    reshape x3 -> x2, local copies, waits for them, and re-layouts: 58.2 us -> 2.96 us  [the longest x1 2.76 us: window_tokens(): return blocks.transpose((3, 1, 0, 2, 4)).reshape((shape[2] // WLON, -1, 1))]
    gather x2 -> x0, local copies, waits for them, and re-layouts: 50.7 us -> none  [on_device(): bias_full = bias_table[:, table_index]]
  transfers between devices with their start and end apart: 8 -> 24, of which waited for: 2 -> 10; matrix products, arithmetic and copies ran while one was open for 36% -> 2% of each run, Pallas kernels for 0% -> 74%
where the time goes in v1:
time: 361 us; the launch traced here: 355 us
  Pallas kernels  270 us (75%)
  waiting for transfers between devices  41.9 us (12%)
  starting transfers between devices  22.3 us (6%)
  local copies, waits for them, and re-layouts  12.5 us (3%)
  between operations  6.02 us (2%)
    pallas_call x4, Pallas kernels, run_block(): pl.pallas_call(functools.partial(block_kernel, begin, halo_first, len(sum...  148 us
    pallas_call x1, Pallas kernels, scattered_sum(): pl.pallas_call(functools.partial(scatter_kernel, lats, leads), out_shape=...  70.2 us
    ppermute x20, waiting for transfers between devices, passed_along(): return lax.ppermute(value, axis, pairs)  39.3 us
    ppermute x20, starting transfers between devices, passed_along(): return lax.ppermute(value, axis, pairs)  21.7 us
    pallas_call x5, Pallas kernels, roll_back(): pl.pallas_call(functools.partial(unroll_kernel, spec, rows), out_shape=(p...  17.9 us
    pallas_call x4, Pallas kernels, roll_in(): pl.pallas_call(functools.partial(roll_kernel, specs, rows), out_shape=out...  11.4 us
  transfers between devices with their start and end apart: 24, of which 10 were waited for; matrix products, arithmetic and copies ran while one was open for 2% of the time, Pallas kernels for 74%

profile of v1, /device:TPU:18, one launch (start us, length us, event | category | flops | bytes accessed | tf_op | source)
XLA Modules:
  0.0 354.8 jit_solution(10111027439286761174)
XLA Ops:
  0.7 1.2 slice.30
  1.9 0.8 fusion.1
  2.7 0.5 collective-permute-start.3
  3.3 0.5 collective-permute-start
  3.8 4.0 %collective-permute-done.refs_0_ = s32[2]{0:T(128)S(1)} collective-permute-done((s32[2]{0:T(128)}, s32[2]{0:T(128)S(1)}, u32[]{:S(2)}, u32[]{:S(2)}) %collective-permute-start) | collective-permute-done | bytes 40 | tf_op jit(solution)/shard_map/ppermute | solution.py:47
  7.8 2.4 collective-permute-done.3.refs_3_
  10.2 2.4 roll_in.4.refs_4_.refs_0_
  12.7 1.5 collective-permute-start.6
  14.2 2.5 slice.31
  16.7 1.6 collective-permute-start.2
  18.3 3.5 margins.1
  21.9 1.7 copy-done.9
  23.6 0.6 fusion.6
  28.8 1.1 fusion.3
  30.0 0.1 fusion
  30.1 0.2 reshape.57
  30.3 0.2 copy.50
  30.5 2.8 reshape.67.live_ref
  33.3 0.6 collective-permute-start.5
  33.8 2.6 roll_in.5.refs_4_.refs_0_.refs_3_
  36.5 1.5 collective-permute-start.4
  38.0 2.6 roll_in.6.refs_4_
  40.6 0.5 collective-permute-start.8
  41.2 2.6 prepare.1
  43.8 3.8 %roll_in.7 = f32[4,432,256]{2,1,0:T(8,128)} custom-call(s32[2]{0:T(128)S(1)} %collective-permute-done.refs_0_, f32[2,18,192,256]{3,2,1,0:T(8,128)} %bitcast.59, f32[2,5,128,256]{3,2,1,0:T(8,128)} %collective-permute-done.2.refs_3_.refs_2_, f32[2,5,64,256]{3,2,1,0:T(8,128)S(1)} %collective-permute-done.1.refs_2_.refs_3_, f32[4,432,256]{2,1,0:T(8,128)S(1)} %roll_in.6.refs_4_), custom_call_target="tpu_custom_call" | custom-call | flops 1 | bytes 1 | tf_op jit(solution)/shard_map/roll_in/pallas_call | solution.py:438
  47.6 0.1 collective-permute-done.7.halo_hbm
  47.8 1.7 collective-permute-start.9
  49.5 4.0 %collective-permute-done.6.recv_ref = f32[4,432,256]{2,1,0:T(8,128)} collective-permute-done((f32[4,432,256]{2,1,0:T(8,128)S(1)}, f32[4,432,256]{2,1,0:T(8,128)}, u32[]{:S(2)}, u32[]{:S(2)}) %collective-permute-start.6) | collective-permute-done | bytes 1769504 | tf_op jit(solution)/shard_map/ppermute | solution.py:47
  53.4 36.2 %block.4 = (f32[4,432,256]{2,1,0:T(8,128)}, f32[4,432,256]{2,1,0:T(8,128)}, f32[4,144,512]{2,1,0:T(8,128)S(1)}, f32[3328,256]{1,0:T(8,128)}, f32[144,1152]{1,0:T(8,128)S(1)}, /*index=5*/f32[8,2560]{1,0:T(8,128)S(1)}) custom-call(s32[2]{0:T(128)S(1)} %bitcast.41, f32[4,432,256]{2,1,0:T(8,128)} %collective-permute-done.6.recv_ref, ...), custom_call_target="tpu_custom_call" | custom-call | flops 40000000000 | bytes 1 | tf_op jit(solution)/shard_map/block/pallas_call | solution.py:1068
  89.6 2.1 collective-permute-start.10
  91.8 37.4 %block.5 = (f32[4,432,256]{2,1,0:T(8,128)}, f32[4,432,256]{2,1,0:T(8,128)}, f32[4,144,512]{2,1,0:T(8,128)S(1)}, f32[3328,256]{1,0:T(8,128)}, f32[144,1152]{1,0:T(8,128)S(1)}, /*index=5*/f32[8,2560]{1,0:T(8,128)S(1)}) custom-call(s32[2]{0:T(128)S(1)} %bitcast.42, ...), custom_call_target="tpu_custom_call", output_to_operand_aliasing={{3}: (18, {}), {4}: (19, {}), {5}: (20, {})} | custom-call | flops 40000000000 | bytes 1 | tf_op jit(solution)/shard_map/block/pallas_call | solution.py:1068
  129.2 2.0 collective-permute-start.11
  131.1 1.1 copy-done.11
  132.2 1.0 copy-done.14
  133.3 1.0 copy-done.17
  134.3 37.4 %block.6 = (f32[4,432,256]{2,1,0:T(8,128)}, f32[4,432,256]{2,1,0:T(8,128)}, f32[4,144,512]{2,1,0:T(8,128)S(1)}, f32[3328,256]{1,0:T(8,128)}, f32[144,1152]{1,0:T(8,128)S(1)}, /*index=5*/f32[8,2560]{1,0:T(8,128)S(1)}) custom-call(s32[2]{0:T(128)S(1)} %bitcast.43, ...), custom_call_target="tpu_custom_call", output_to_operand_aliasing={{3}: (18, {}), {4}: (19, {}), {5}: (20, {})} | custom-call | flops 40000000000 | bytes 1 | tf_op jit(solution)/shard_map/block/pallas_call | solution.py:1068
  171.6 2.1 collective-permute-start.12
  173.7 4.3 %roll_back.5.refs_3_ = f32[2,18,80,256]{3,2,1,0:T(8,128)} custom-call(s32[2]{0:T(128)S(1)} %bitcast.44, f32[4,432,256]{2,1,0:T(8,128)} %get-tuple-element.78.refs_1_.refs_2_.refs_3_.refs_4_.refs_6_.refs_7_, f32[4,432,256]{2,1,0:T(8,128)} %get-tuple-element.78.refs_1_.refs_2_.refs_3_.refs_4_.refs_6_.refs_7_, ...), custom_call_target="tpu_custom_call" | custom-call | flops 1 | bytes 1 | tf_op jit(solution)/shard_map/roll_back/pallas_call | solution.py:556
  178.0 1.6 collective-permute-start.14
  179.6 37.5 %block.7 = (f32[4,432,256]{2,1,0:T(8,128)}, f32[4,432,256]{2,1,0:T(8,128)}, f32[4,144,512]{2,1,0:T(8,128)S(1)}, f32[3328,256]{1,0:T(8,128)}, f32[144,1152]{1,0:T(8,128)S(1)}, /*index=5*/f32[8,2560]{1,0:T(8,128)S(1)}) custom-call(s32[2]{0:T(128)S(1)} %bitcast.45, ...), custom_call_target="tpu_custom_call", output_to_operand_aliasing={{3}: (18, {}), {4}: (19, {}), {5}: (20, {})} | custom-call | flops 40000000000 | bytes 1 | tf_op jit(solution)/shard_map/block/pallas_call | solution.py:1068
  217.1 2.1 roll_back.6.refs_1_
  219.2 1.6 collective-permute-start.15
  220.9 1.1 collective-permute-start.13
  221.9 3.4 collect.1.in_ref
  225.4 70.2 %scattered_sum.1.refs_15_.refs_0_ = f32[416,256]{1,0:T(8,128)S(1)} custom-call(f32[3328,256]{1,0:T(8,128)S(1)} %collect.1.in_ref), custom_call_target="tpu_custom_call" | custom-call | flops 1 | bytes 1 | tf_op jit(solution)/shard_map/scattered_sum/pallas_call | solution.py:255
  295.6 2.3 roll_back.7.refs_17_
  297.9 0.6 collective-permute-start.16
  298.5 0.4 collective-permute-start.17
  299.0 1.6 collective-permute-start.19
  300.6 4.1 %roll_back.8.refs_23_ = f32[2,18,192,256]{3,2,1,0:T(8,128)} custom-call(s32[2]{0:T(128)S(1)} %bitcast.48, f32[4,432,256]{2,1,0:T(8,128)} %get-tuple-element.83.refs_1_.refs_2_.refs_3_.refs_4_.refs_10_.refs_11_, f32[4,432,256]{2,1,0:T(8,128)} %get-tuple-element.83.refs_1_.refs_2_.refs_3_.refs_4_.refs_10_.refs_11_, ...), custom_call_target="tpu_custom_call" | custom-call | flops 1 | bytes 1 | tf_op jit(solution)/shard_map/roll_back/pallas_call | solution.py:556
  304.7 5.1 %roll_back.9.refs_0_ = f32[2,18,192,256]{3,2,1,0:T(8,128)} custom-call(s32[2]{0:T(128)S(1)} %bitcast.49, f32[4,432,256]{2,1,0:T(8,128)} %get-tuple-element.70.refs_5_.refs_6_.refs_7_.refs_8_.refs_1_, f32[4,432,256]{2,1,0:T(8,128)} %get-tuple-element.74.refs_2_.refs_3_.refs_4_.refs_5_, ...), custom_call_target="tpu_custom_call", output_to_operand_aliasing={{}: (23, {})} | custom-call | flops 1 | bytes 1 | tf_op jit(solution)/shard_map/roll_back/pallas_call | solution.py:556
  309.7 2.3 place.3.refs_0_
  312.1 1.6 place.4.refs_0_.refs_3_
  313.7 15.8 %collective-permute-done.17.refs_0_ = f32[416,256]{1,0:T(8,128)S(1)} collective-permute-done((f32[416,256]{1,0:T(8,128)S(1)}, f32[416,256]{1,0:T(8,128)S(1)}, u32[]{:S(2)}, u32[]{:S(2)}) %collective-permute-start.17) | collective-permute-done | bytes 426016 | tf_op jit(solution)/shard_map/ppermute | solution.py:47
  329.5 4.1 %collective-permute-done.19.refs_2_ = f32[416,256]{1,0:T(8,128)S(1)} collective-permute-done((f32[416,256]{1,0:T(8,128)S(1)}, f32[416,256]{1,0:T(8,128)S(1)}, u32[]{:S(2)}, u32[]{:S(2)}) %collective-permute-start.19) | collective-permute-done | bytes 426016 | tf_op jit(solution)/shard_map/ppermute | solution.py:47
  333.7 1.1 hold.1
  334.8 0.5 collective-permute-start.22
  335.4 0.1 copy.55
  335.5 1.4 collective-permute-done.21.refs_5_
  336.9 0.6 collective-permute-done.22.refs_6_
  337.5 0.6 collective-permute-done.23.refs_7_
  338.2 4.8 %finish.1 = (f32[256,512]{1,0:T(8,128)}, f32[1,512]{1,0:T(1,128)}, f32[256,768]{1,0:T(8,128)}, f32[8,759]{1,0:T(8,128)}, f32[256,256]{1,0:T(8,128)}, /*index=5*/...) custom-call(s32[2]{0:T(128)S(1)} %pad_add_fusion.place_ref, ...), custom_call_target="tpu_custom_call" | custom-call | flops 1 | bytes 1 | tf_op jit(solution)/shard_map/finish/pallas_call | solution.py:359
  343.0 8.8 %collective-permute-done.16.piece_hbm = f32[2,18,64,256]{3,2,1,0:T(8,128)} collective-permute-done((f32[2,18,64,256]{3,2,1,0:T(8,128)S(1)}, f32[2,18,64,256]{3,2,1,0:T(8,128)}, u32[]{:S(2)}, u32[]{:S(2)}) %collective-permute-start.16) | collective-permute-done | bytes 2359328 | tf_op jit(solution)/shard_map/ppermute | solution.py:47
  351.8 2.8 place.5
  (83 shorter events, 0.5 us)
Async XLA Ops:
  0.6 28.1 %copy-start = (f32[256,512]{1,0:T(8,128)S(1)}, f32[256,512]{1,0:T(8,128)}, u32[]{:S(2)}) copy-start(f32[256,512]{1,0:T(8,128)} %param.26) | copy-start | bytes 1572868
  1.9 8.3 %collective-permute-start.1 = (f32[2,5,64,256]{3,2,1,0:T(8,128)S(1)}, f32[2,5,64,256]{3,2,1,0:T(8,128)S(1)}, u32[]{:S(2)}, u32[]{:S(2)}) collective-permute-start(f32[2,5,64,256]{3,2,1,0:T(8,128)S(1)} %slice.30), channel_id=1, source_target_pairs={{0,7},{1,0},{2,1},{3,2},{4,3},{5,4},{6,5},{7,6},{8,15},{9,8},{10,9... | collective-permute-start | bytes 1966088 | tf_op jit(solution)/shard_map/ppermute | solution.py:47
  2.7 7.5 %collective-permute-start.3 = (f32[2,5,192]{2,1,0:T(8,128)S(1)}, f32[2,5,192]{2,1,0:T(8,128)S(1)}, u32[]{:S(2)}, u32[]{:S(2)}) collective-permute-start(f32[2,5,192]{2,1,0:T(8,128)S(1)} %slice.32), channel_id=1, source_target_pairs={{0,7},{1,0},{2,1},{3,2},{4,3},{5,4},{6,5},{7,6},{8,15},{9,8},{10,9... | collective-permute-start | bytes 23048 | tf_op jit(solution)/shard_map/ppermute | solution.py:47
  3.3 4.6 %collective-permute-start = (s32[2]{0:T(128)}, s32[2]{0:T(128)S(1)}, u32[]{:S(2)}, u32[]{:S(2)}) collective-permute-start(s32[2]{0:T(128)} %bitcast.40), channel_id=1, source_target_pairs={{0,24},{8,0},{16,8},{24,16},{1,25},{9,1},{17,9},{25,17},{2,26},{10... | collective-permute-start | bytes 32 | tf_op jit(solution)/shard_map/ppermute | solution.py:47
  12.7 40.8 %collective-permute-start.6 = (f32[4,432,256]{2,1,0:T(8,128)S(1)}, f32[4,432,256]{2,1,0:T(8,128)}, u32[]{:S(2)}, u32[]{:S(2)}) collective-permute-start(f32[4,432,256]{2,1,0:T(8,128)S(1)} %roll_in.4.refs_4_.refs_0_), channel_id=1, source_target_pairs={{0,8},{8,16},{16,24},{24,0},{1,9},{9,17},{17,25},{25,1},{2,10},{10... | collective-permute-start | bytes 5308424 | tf_op jit(solution)/shard_map/ppermute | solution.py:47
  16.7 17.2 %collective-permute-start.2 = (f32[2,5,128,256]{3,2,1,0:T(8,128)}, f32[2,5,128,256]{3,2,1,0:T(8,128)}, u32[]{:S(2)}, u32[]{:S(2)}) collective-permute-start(f32[2,5,128,256]{3,2,1,0:T(8,128)} %slice.31), channel_id=1, source_target_pairs={{0,7},{1,0},{2,1},{3,2},{4,3},{5,4},{6,5},{7,6},{8,15},{9,8},{10,9... | collective-permute-start | bytes 3932168 | tf_op jit(solution)/shard_map/ppermute | solution.py:47
  18.3 5.3 %copy-start.8 = (s32[1,2]{1,0:T(1,128)S(1)}, s32[1,2]{1,0:T(1,128)}, u32[]{:S(2)}) copy-start(s32[1,2]{1,0:T(1,128)} %param.23) | copy-start | bytes 28
  18.3 11.5 %copy-start.24 = (f32[512]{0:T(512)S(1)}, f32[512]{0:T(512)}, u32[]{:S(2)}) copy-start(f32[512]{0:T(512)} %param.27) | copy-start | bytes 6148
  18.3 11.5 %copy-start.22 = (f32[8,759]{1,0:T(8,128)S(1)}, f32[8,759]{1,0:T(8,128)}, u32[]{:S(2)}) copy-start(f32[8,759]{1,0:T(8,128)} %param.29) | copy-start | bytes 72868
  18.3 11.6 %copy-start.25 = (f32[256]{0:T(256)S(1)}, f32[256]{0:T(256)}, u32[]{:S(2)}) copy-start(f32[256]{0:T(256)} %param.37) | copy-start | bytes 3076
  18.3 11.6 %copy-start.26 = (f32[256]{0:T(256)S(1)}, f32[256]{0:T(256)}, u32[]{:S(2)}) copy-start(f32[256]{0:T(256)} %param.33) | copy-start | bytes 3076
  18.3 11.6 %copy-start.27 = (f32[256]{0:T(256)S(1)}, f32[256]{0:T(256)}, u32[]{:S(2)}) copy-start(f32[256]{0:T(256)} %param.32) | copy-start | bytes 3076
  18.3 11.6 %copy-start.28 = (f32[256]{0:T(256)S(1)}, f32[256]{0:T(256)}, u32[]{:S(2)}) copy-start(f32[256]{0:T(256)} %param.31) | copy-start | bytes 3076
  21.9 1.7 copy-start.9
  23.6 24.2 %collective-permute-start.7 = (f32[2,2,5,64,256]{4,3,2,1,0:T(8,128)}, f32[2,2,5,64,256]{4,3,2,1,0:T(8,128)}, u32[]{:S(2)}, u32[]{:S(2)}) collective-permute-start(f32[2,2,5,64,256]{4,3,2,1,0:T(8,128)} %get-tuple-element.66), channel_id=1, source_target_pairs={{0,7},{1,0},{2,1},{3,2},{4,3},{5,4},{6,5},{7,6},{8,15},{9,8},{10,9... | collective-permute-start | bytes 3932168 | tf_op jit(solution)/shard_map/ppermute | solution.py:47
  33.3 58.5 %collective-permute-start.5 = (f32[2,2,5,160,256]{4,3,2,1,0:T(8,128)}, f32[2,2,5,160,256]{4,3,2,1,0:T(8,128)}, u32[]{:S(2)}, u32[]{:S(2)}) collective-permute-start(f32[2,2,5,160,256]{4,3,2,1,0:T(8,128)} %copy-done.9), channel_id=1, source_target_pairs={{0,7},{1,0},{2,1},{3,2},{4,3},{5,4},{6,5},{7,6},{8,15},{9,8},{10,9... | collective-permute-start | bytes 9830408 | tf_op jit(solution)/shard_map/ppermute | solution.py:47
  36.4 4.7 %copy-start.2 = (f32[4,432,256]{2,1,0:T(8,128)}, f32[4,432,256]{2,1,0:T(8,128)S(1)}, u32[]{:S(2)}) copy-start(f32[4,432,256]{2,1,0:T(8,128)S(1)} %roll_in.5.refs_4_.refs_0_.refs_3_) | copy-start | bytes 5308420
  36.4 4.7 %copy-start.4 = (bf16[256,1024]{1,0:T(8,128)(2,1)S(1)}, bf16[256,1024]{1,0:T(8,128)(2,1)}, u32[]{:S(2)}) copy-start(bf16[256,1024]{1,0:T(8,128)(2,1)} %w_up_ref.7) | copy-start | bytes 1572868
  36.4 4.7 %copy-start.5 = (bf16[1024,256]{1,0:T(8,128)(2,1)S(1)}, bf16[1024,256]{1,0:T(8,128)(2,1)}, u32[]{:S(2)}) copy-start(bf16[1024,256]{1,0:T(8,128)(2,1)} %w_down_ref.7) | copy-start | bytes 1572868
  36.5 4.7 %copy-start.6 = (bf16[256,768]{1,0:T(8,128)(2,1)S(1)}, bf16[256,768]{1,0:T(8,128)(2,1)}, u32[]{:S(2)}) copy-start(bf16[256,768]{1,0:T(8,128)(2,1)} %w_qkv_ref.7) | copy-start | bytes 1179652
  36.5 4.7 %copy-start.7 = (bf16[256,256]{1,0:T(8,128)(2,1)S(1)}, bf16[256,256]{1,0:T(8,128)(2,1)}, u32[]{:S(2)}) copy-start(bf16[256,256]{1,0:T(8,128)(2,1)} %w_out_ref.7) | copy-start | bytes 393220
  36.5 55.3 %collective-permute-start.4 = (f32[4,432,256]{2,1,0:T(8,128)S(1)}, f32[4,432,256]{2,1,0:T(8,128)}, u32[]{:S(2)}, u32[]{:S(2)}) collective-permute-start(f32[4,432,256]{2,1,0:T(8,128)S(1)} %roll_in.5.refs_4_.refs_0_.refs_3_), channel_id=1, source_target_pairs={{0,8},{8,16},{16,24},{24,0},{1,9},{9,17},{17,25},{25,1},{2,10},{10... | collective-permute-start | bytes 5308424 | tf_op jit(solution)/shard_map/ppermute | solution.py:47
  40.6 90.5 %collective-permute-start.8 = (f32[4,432,256]{2,1,0:T(8,128)S(1)}, f32[4,432,256]{2,1,0:T(8,128)}, u32[]{:S(2)}, u32[]{:S(2)}) collective-permute-start(f32[4,432,256]{2,1,0:T(8,128)S(1)} %roll_in.6.refs_4_), channel_id=1, source_target_pairs={{0,8},{8,16},{16,24},{24,0},{1,9},{9,17},{17,25},{25,1},{2,10},{10... | collective-permute-start | bytes 5308424 | tf_op jit(solution)/shard_map/ppermute | solution.py:47
  43.8 48.0 %copy-start.10 = (f32[144,1152]{1,0:T(8,128)}, f32[144,1152]{1,0:T(8,128)S(1)}, u32[]{:S(2)}) copy-start(f32[144,1152]{1,0:T(8,128)S(1)} %get-tuple-element.62.bias_ref) | copy-start | bytes 1990660
  43.8 48.0 %copy-start.13 = (bf16[256,1024]{1,0:T(8,128)(2,1)}, bf16[256,1024]{1,0:T(8,128)(2,1)S(1)}, u32[]{:S(2)}) copy-start(bf16[256,1024]{1,0:T(8,128)(2,1)S(1)} %get-tuple-element.65.w_down_t_ref) | copy-start | bytes 1572868
  43.8 48.0 %copy-start.16 = (bf16[768,256]{1,0:T(8,128)(2,1)}, bf16[768,256]{1,0:T(8,128)(2,1)S(1)}, u32[]{:S(2)}) copy-start(bf16[768,256]{1,0:T(8,128)(2,1)S(1)} %get-tuple-element.61.w_qkv_t_ref) | copy-start | bytes 1179652
  43.8 87.3 %copy-start.19 = (bf16[256,256]{1,0:T(8,128)(2,1)}, bf16[256,256]{1,0:T(8,128)(2,1)S(1)}, u32[]{:S(2)}) copy-start(bf16[256,256]{1,0:T(8,128)(2,1)S(1)} %get-tuple-element.63.w_out_t_ref) | copy-start | bytes 393220
  43.8 9.6 %copy-start.21 = (f32[1024]{0:T(1024)S(1)}, f32[1024]{0:T(1024)}, u32[]{:S(2)}) copy-start(f32[1024]{0:T(1024)} %param.35) | copy-start | bytes 12292
  47.8 131.8 %collective-permute-start.9 = (f32[4,432,256]{2,1,0:T(8,128)}, f32[4,432,256]{2,1,0:T(8,128)}, u32[]{:S(2)}, u32[]{:S(2)}) collective-permute-start(f32[4,432,256]{2,1,0:T(8,128)} %roll_in.7), channel_id=1, source_target_pairs={{0,8},{8,16},{16,24},{24,0},{1,9},{9,17},{17,25},{25,1},{2,10},{10... | collective-permute-start | bytes 5308424 | tf_op jit(solution)/shard_map/ppermute | solution.py:47
  89.6 84.1 %collective-permute-start.10 = (f32[4,144,512]{2,1,0:T(8,128)S(1)}, f32[4,144,512]{2,1,0:T(8,128)S(1)}, u32[]{:S(2)}, u32[]{:S(2)}) collective-permute-start(f32[4,144,512]{2,1,0:T(8,128)S(1)} %get-tuple-element.80), channel_id=1, source_target_pairs={{0,1},{1,2},{2,3},{3,4},{4,5},{5,6},{6,7},{7,0},{8,9},{9,10},{10,1... | collective-permute-start | bytes 3538952 | tf_op jit(solution)/shard_map/ppermute | solution.py:47
  129.2 44.5 %collective-permute-start.11 = (f32[4,144,512]{2,1,0:T(8,128)S(1)}, f32[4,144,512]{2,1,0:T(8,128)S(1)}, u32[]{:S(2)}, u32[]{:S(2)}) collective-permute-start(f32[4,144,512]{2,1,0:T(8,128)S(1)} %get-tuple-element.81), channel_id=1, source_target_pairs={{0,1},{1,2},{2,3},{3,4},{4,5},{5,6},{6,7},{7,0},{8,9},{9,10},{10,1... | collective-permute-start | bytes 3538952 | tf_op jit(solution)/shard_map/ppermute | solution.py:47
  131.1 1.1 copy-start.11
  132.2 1.0 copy-start.14
  133.3 1.0 copy-start.17
  171.6 45.5 %collective-permute-start.12 = (f32[4,144,512]{2,1,0:T(8,128)S(1)}, f32[4,144,512]{2,1,0:T(8,128)S(1)}, u32[]{:S(2)}, u32[]{:S(2)}) collective-permute-start(f32[4,144,512]{2,1,0:T(8,128)S(1)} %get-tuple-element.84), channel_id=1, source_target_pairs={{0,1},{1,2},{2,3},{3,4},{4,5},{5,6},{6,7},{7,0},{8,9},{9,10},{10,1... | collective-permute-start | bytes 3538952 | tf_op jit(solution)/shard_map/ppermute | solution.py:47
  173.7 5.9 %copy-start.12 = (f32[144,1152]{1,0:T(8,128)S(1)}, f32[144,1152]{1,0:T(8,128)}, u32[]{:S(2)}) copy-start(f32[144,1152]{1,0:T(8,128)} %copy-done.10) | copy-start | bytes 1990660
  173.7 5.9 %copy-start.15 = (bf16[256,1024]{1,0:T(8,128)(2,1)S(1)}, bf16[256,1024]{1,0:T(8,128)(2,1)}, u32[]{:S(2)}) copy-start(bf16[256,1024]{1,0:T(8,128)(2,1)} %copy-done.13) | copy-start | bytes 1572868
  173.7 5.9 %copy-start.18 = (bf16[768,256]{1,0:T(8,128)(2,1)S(1)}, bf16[768,256]{1,0:T(8,128)(2,1)}, u32[]{:S(2)}) copy-start(bf16[768,256]{1,0:T(8,128)(2,1)} %copy-done.16) | copy-start | bytes 1179652
  173.7 5.9 %copy-start.20 = (bf16[256,256]{1,0:T(8,128)(2,1)S(1)}, bf16[256,256]{1,0:T(8,128)(2,1)}, u32[]{:S(2)}) copy-start(bf16[256,256]{1,0:T(8,128)(2,1)} %copy-done.19) | copy-start | bytes 393220
  178.0 117.5 %collective-permute-start.14 = (f32[2,18,80,256]{3,2,1,0:T(8,128)}, f32[2,18,80,256]{3,2,1,0:T(8,128)S(1)}, u32[]{:S(2)}, u32[]{:S(2)}) collective-permute-start(f32[2,18,80,256]{3,2,1,0:T(8,128)} %roll_back.5.refs_3_), channel_id=1, source_target_pairs={{0,24},{8,0},{16,8},{24,16},{1,25},{9,1},{17,9},{25,17},{2,26},{10... | collective-permute-start | bytes 8847368 | tf_op jit(solution)/shard_map/ppermute | solution.py:47
  217.1 4.8 %copy-start.3 = (f32[3328,256]{1,0:T(8,128)S(1)}, f32[3328,256]{1,0:T(8,128)}, u32[]{:S(2)}) copy-start(f32[3328,256]{1,0:T(8,128)} %get-tuple-element.90.refs_0_) | copy-start | bytes 10223620
  219.2 76.3 %collective-permute-start.15 = (f32[2,18,48,256]{3,2,1,0:T(8,128)S(1)}, f32[2,18,48,256]{3,2,1,0:T(8,128)S(1)}, u32[]{:S(2)}, u32[]{:S(2)}) collective-permute-start(f32[2,18,48,256]{3,2,1,0:T(8,128)S(1)} %roll_back.6.refs_1_), channel_id=1, source_target_pairs={{0,24},{8,0},{16,8},{24,16},{1,25},{9,1},{17,9},{25,17},{2,26},{10... | collective-permute-start | bytes 5308424 | tf_op jit(solution)/shard_map/ppermute | solution.py:47
  220.9 74.7 %collective-permute-start.13 = (f32[4,144,512]{2,1,0:T(8,128)S(1)}, f32[4,144,512]{2,1,0:T(8,128)S(1)}, u32[]{:S(2)}, u32[]{:S(2)}) collective-permute-start(f32[4,144,512]{2,1,0:T(8,128)S(1)} %get-tuple-element.85), channel_id=1, source_target_pairs={{0,1},{1,2},{2,3},{3,4},{4,5},{5,6},{6,7},{7,0},{8,9},{9,10},{10,1... | collective-permute-start | bytes 3538952 | tf_op jit(solution)/shard_map/ppermute | solution.py:47
  297.9 53.9 %collective-permute-start.16 = (f32[2,18,64,256]{3,2,1,0:T(8,128)S(1)}, f32[2,18,64,256]{3,2,1,0:T(8,128)}, u32[]{:S(2)}, u32[]{:S(2)}) collective-permute-start(f32[2,18,64,256]{3,2,1,0:T(8,128)S(1)} %roll_back.7.refs_17_), channel_id=1, source_target_pairs={{0,24},{8,0},{16,8},{24,16},{1,25},{9,1},{17,9},{25,17},{2,26},{10... | collective-permute-start | bytes 7077896 | tf_op jit(solution)/shard_map/ppermute | solution.py:47
  298.5 31.0 %collective-permute-start.17 = (f32[416,256]{1,0:T(8,128)S(1)}, f32[416,256]{1,0:T(8,128)S(1)}, u32[]{:S(2)}, u32[]{:S(2)}) collective-permute-start(f32[416,256]{1,0:T(8,128)S(1)} %scattered_sum.1.refs_15_.refs_0_), channel_id=1, source_target_pairs={{0,2},{1,3},{2,4},{3,5},{4,6},{5,7},{6,0},{7,1},{8,10},{9,11},{10,... | collective-permute-start | bytes 1277960 | tf_op jit(solution)/shard_map/ppermute | solution.py:47
  299.0 30.6 %collective-permute-start.18 = (f32[416,256]{1,0:T(8,128)S(1)}, f32[416,256]{1,0:T(8,128)S(1)}, u32[]{:S(2)}, u32[]{:S(2)}) collective-permute-start(f32[416,256]{1,0:T(8,128)S(1)} %scattered_sum.1.refs_15_.refs_0_), channel_id=1, source_target_pairs={{0,4},{1,5},{2,6},{3,7},{4,0},{5,1},{6,2},{7,3},{8,12},{9,13},{10,... | collective-permute-start | bytes 1277960 | tf_op jit(solution)/shard_map/ppermute | solution.py:47
  299.0 34.7 %collective-permute-start.19 = (f32[416,256]{1,0:T(8,128)S(1)}, f32[416,256]{1,0:T(8,128)S(1)}, u32[]{:S(2)}, u32[]{:S(2)}) collective-permute-start(f32[416,256]{1,0:T(8,128)S(1)} %scattered_sum.1.refs_15_.refs_0_), channel_id=1, source_target_pairs={{0,6},{1,7},{2,0},{3,1},{4,2},{5,3},{6,4},{7,5},{8,14},{9,15},{10,... | collective-permute-start | bytes 1277960 | tf_op jit(solution)/shard_map/ppermute | solution.py:47
  312.0 23.5 %collective-permute-start.20 = (f32[416,256]{1,0:T(8,128)S(1)}, f32[416,256]{1,0:T(8,128)S(1)}, u32[]{:S(2)}, u32[]{:S(2)}) collective-permute-start(f32[416,256]{1,0:T(8,128)S(1)} %scattered_sum.1.refs_15_.refs_0_), channel_id=1, source_target_pairs={{0,1},{1,0},{2,3},{3,2},{4,5},{5,4},{6,7},{7,6},{8,9},{9,8},{10,11... | collective-permute-start | bytes 1277960 | tf_op jit(solution)/shard_map/ppermute | solution.py:299
  313.7 21.6 %copy-start.23 = (f32[16,256]{1,0:T(8,128)S(1)}, f32[16,256]{1,0:T(8,128)}, u32[]{:S(2)}) copy-start(f32[16,256]{1,0:T(8,128)} %param.25) | copy-start | bytes 49156
  334.8 2.1 collective-permute-start.21
  334.8 2.7 collective-permute-start.22
  335.3 2.8 collective-permute-start.23
  351.8 2.8 copy-start.1

commit v2 on v1

--- a/solution.py
+++ b/solution.py
@@ -38,7 +38,7 @@
 ANYWHERE = pl.BlockSpec(memory_space=pl.ANY)
 SMALL = pl.CostEstimate(flops=1, bytes_accessed=1, transcendentals=0)
 LIMIT = 30 * 1024 * 1024
-BLOCK_LIMIT = 48 * 1024 * 1024
+BLOCK_LIMIT = 62 * 1024 * 1024
 
 
 def passed_along(value, axis, steps):
@@ -88,8 +88,8 @@
     padded = jnp.pad(bias_table, ((0, 0), (0, TABLE_PAD - TABLE_ROWS)))
     return pl.pallas_call(
         functools.partial(prepare_kernel, len(weights)),
-        out_shape=[jax.ShapeDtypeStruct((SPAN, HEADS * SPAN), F32)]
-        + [jax.ShapeDtypeStruct(array.shape[::-1], array.dtype) for array in weights],
+        out_shape=[pltpu.HBM((SPAN, HEADS * SPAN), F32)]
+        + [pltpu.HBM(array.shape[::-1], array.dtype) for array in weights],
         in_specs=[WHOLE] * (1 + len(weights)) + [ANYWHERE] * len(after),
         out_specs=[WHOLE] * (1 + len(weights)),
         scratch_shapes=[VMEM((HEADS, SPAN, TABLE_PAD), F32)],
@@ -1185,17 +1185,17 @@
     )
     fixed = [
         mod,
-        w_qkv,
-        w_qkv_t,
-        bias,
-        w_out,
-        w_out_t,
+        in_hbm(w_qkv),
+        in_hbm(w_qkv_t),
+        in_hbm(bias),
+        in_hbm(w_out),
+        in_hbm(w_out_t),
         vectors,
-        w_up,
-        w_up_t,
+        in_hbm(w_up),
+        in_hbm(w_up_t),
         b_up[None],
-        w_down,
-        w_down_t,
+        in_hbm(w_down),
+        in_hbm(w_down_t),
     ]
     main_rows = 4 * width + 2 * hidden
     few = 6 * width + hidden
@@ -1217,9 +1217,14 @@
         own, tail = zip(*picked)
         return roll_back(offsets, own, tail, low * WLON, start, end, shape, after, into)
 
-    bounds = [(end * WLON + 1) // 16 * 16 for end in ends[:-1]] + [cols + 16]
+    bounds = [(end * WLON + 1) // 8 * 8 for end in ends[:-1]] + [cols + 16]
     pieces = list(zip([16] + bounds[:-1], bounds))
-    rolled, grad_pieces = [], []
+    rolled, sent = [], []
+
+    def send(start, end, after):
+        rolled.append(back(grads, start, end, after))
+        sent.append((passed_along(rolled[-1], "lead", -1), start))
+
     for index, (begin, end) in enumerate(steps):
         made = run_block(
             offsets,
@@ -1241,20 +1246,23 @@
             results.append(((made[0], window - begin), (tail, window - begin, 0)))
             grads.append(((made[1], window - begin), (tail, window - begin, 1)))
         if index == len(steps) - 2:
-            rolled.append(back(grads, pieces[0][0], pieces[index - 1][1], [made[4]]))
-            grad_pieces.append(passed_along(rolled[-1], "lead", -1))
-    rolled.append(back(grads, *pieces[-2], [made[4]]))
-    grad_pieces.append(passed_along(rolled[-1], "lead", -1))
+            send(pieces[0][0], pieces[index - 1][1], [made[4]])
+    send(*pieces[-2], [made[4]])
     buffer = collect(lead_index, embeddings.shape[0], sums[1], sums[2], sums[0], main_rows, rolled[-1:])
     part = scattered_sum(buffer, [])
-    rolled.append(back(grads, *pieces[-1], [part] + grad_pieces))
-    grad_pieces.append(passed_along(rolled[-1], "lead", -1))
+    early = len(sent)
+    middle = (pieces[-1][0] + pieces[-1][1]) // 16 * 8
+    send(pieces[-1][0], middle, [part] + [piece for piece, _ in sent])
+    send(middle, pieces[-1][1], rolled[-1:])
     block_out = back(results, pieces[0][0], pieces[-3][1], rolled[-1:], (None,))
     block_out = back(results, pieces[-2][0], pieces[-1][1], [], (block_out,))
-    state_grad = placed_in(None, grad_pieces[0], pieces[0][0], shape, [in_hbm(block_out)])
-    state_grad = placed_in(state_grad, grad_pieces[1], pieces[-2][0], shape, [])
+    state_grad, after = None, [in_hbm(block_out)]
+    for piece, start in sent[:early]:
+        state_grad = placed_in(state_grad, piece, start, shape, after)
+        after = []
     own, others = gathered(part, [in_hbm(state_grad)])
-    state_grad = placed_in(state_grad, grad_pieces[2], pieces[-1][0], shape, [])
+    for piece, start in sent[early:]:
+        state_grad = placed_in(state_grad, piece, start, shape, [])
     outs = finished(own, others, embeddings, width, hidden)
     return (block_out[None], state_grad[None]) + outs
 

time: 361 us -> 363 us (level)
  the two profiles are of different devices: /device:TPU:18 before, /device:TPU:10 now
where the time goes in v2:
time: 363 us; the launch traced here: 357 us
  Pallas kernels  279 us (77%)
  waiting for transfers between devices  32.8 us (9%)
  starting transfers between devices  26.1 us (7%)
  local copies, waits for them, and re-layouts  9.88 us (3%)
  between operations  5.93 us (2%)
    pallas_call x4, Pallas kernels, run_block(): pl.pallas_call(functools.partial(block_kernel, begin, halo_first, len(sum...  151 us
    pallas_call x1, Pallas kernels, scattered_sum(): pl.pallas_call(functools.partial(scatter_kernel, lats, leads), out_shape=...  68.9 us
    ppermute x21, waiting for transfers between devices, passed_along(): return lax.ppermute(value, axis, pairs)  30.7 us
    ppermute x21, starting transfers between devices, passed_along(): return lax.ppermute(value, axis, pairs)  25 us
    pallas_call x6, Pallas kernels, roll_back(): pl.pallas_call(functools.partial(unroll_kernel, spec, rows), out_shape=(p...  20.9 us
    pallas_call x4, Pallas kernels, roll_in(): pl.pallas_call(functools.partial(roll_kernel, specs, rows), out_shape=out...  14.7 us
    pallas_call x4, Pallas kernels, placed_in(): pl.pallas_call(functools.partial(place_kernel, targets), out_shape=pltpu....  8.95 us
  transfers between devices with their start and end apart: 25, of which 7 were waited for; matrix products, arithmetic and copies ran while one was open for 3% of the time, Pallas kernels for 77%

profile of v2, /device:TPU:10, one launch (start us, length us, event | category | flops | bytes accessed | tf_op | source)
XLA Modules:
  0.0 357.3 jit_solution(14044741029495711823)
XLA Ops:
  0.7 1.2 slice.30
  1.9 0.8 fusion.1
  2.7 0.5 collective-permute-start.3
  3.3 4.5 %collective-permute-done.refs_0_ = s32[2]{0:T(128)S(1)} collective-permute-done((s32[2]{0:T(128)}, s32[2]{0:T(128)S(1)}, u32[]{:S(2)}, u32[]{:S(2)}) %collective-permute-start) | collective-permute-done | bytes 40 | tf_op jit(solution)/shard_map/ppermute | solution.py:47
  7.8 2.4 collective-permute-done.3.refs_3_
  10.2 3.6 %roll_in.4.refs_4_.refs_0_ = f32[4,432,256]{2,1,0:T(8,128)} custom-call(s32[2]{0:T(128)S(1)} %collective-permute-done.refs_0_, f32[2,18,192,256]{3,2,1,0:T(8,128)} %bitcast.53, f32[2,5,64,256]{3,2,1,0:T(8,128)S(1)} %collective-permute-done.1.refs_2_.refs_3_, f32[2,5,192]{2,1,0:T(8,128)S(1)} %collective-permute-done.3.refs_3_), custom_call_target="tpu_custom_call" | custom-call | flops 1 | bytes 1 | tf_op jit(solution)/shard_map/roll_in/pallas_call | solution.py:438
  13.9 1.5 collective-permute-start.6
  15.4 2.6 slice.31
  18.0 1.6 collective-permute-start.2
  19.6 3.5 margins.1
  23.1 2.0 collective-permute-start.7
  25.2 0.6 fusion.6
  30.3 1.1 fusion.3
  31.4 0.6 pad_maximum_fusion.1.mod_ref
  32.0 0.6 pad_maximum_fusion.vec_ref
  32.6 0.1 fusion
  32.8 0.2 reshape.57
  33.0 0.2 copy.51
  33.2 2.8 reshape.67.live_ref
  35.9 3.4 collective-permute-start.5
  39.4 3.7 %roll_in.5.refs_4_.refs_0_.refs_3_ = f32[4,432,256]{2,1,0:T(8,128)} custom-call(s32[2]{0:T(128)S(1)} %collective-permute-done.refs_0_, f32[2,18,192,256]{3,2,1,0:T(8,128)} %bitcast.55, f32[2,5,64,256]{3,2,1,0:T(8,128)S(1)} %collective-permute-done.1.refs_2_.refs_3_, f32[2,5,128,256]{3,2,1,0:T(8,128)S(1)} %collective-permute-done.2.refs_3_.refs_2_, ...), custom_call_target="tpu_custom_call" | custom-call | flops 1 | bytes 1 | tf_op jit(solution)/shard_map/roll_in/pallas_call | solution.py:438
  43.1 1.5 collective-permute-start.4
  44.7 3.7 %roll_in.6.refs_4_ = f32[4,432,256]{2,1,0:T(8,128)} custom-call(s32[2]{0:T(128)S(1)} %collective-permute-done.refs_0_, f32[2,18,192,256]{3,2,1,0:T(8,128)} %bitcast.56, f32[2,5,128,256]{3,2,1,0:T(8,128)S(1)} %collective-permute-done.2.refs_3_.refs_2_, f32[4,432,256]{2,1,0:T(8,128)} %roll_in.5.refs_4_.refs_0_.refs_3_), custom_call_target="tpu_custom_call" | custom-call | flops 1 | bytes 1 | tf_op jit(solution)/shard_map/roll_in/pallas_call | solution.py:438
  48.4 0.5 collective-permute-start.8
  48.9 3.4 prepare.1
  52.3 3.6 %roll_in.7 = f32[4,432,256]{2,1,0:T(8,128)} custom-call(s32[2]{0:T(128)S(1)} %collective-permute-done.refs_0_, f32[2,18,192,256]{3,2,1,0:T(8,128)} %bitcast.57, f32[2,5,128,256]{3,2,1,0:T(8,128)S(1)} %collective-permute-done.2.refs_3_.refs_2_, f32[2,5,64,256]{3,2,1,0:T(8,128)S(1)} %collective-permute-done.1.refs_2_.refs_3_, f32[4,432,256]{2,1,0:T(8,128)} %roll_in.6.refs_4_), custom_call_target="tpu_custom_call" | custom-call | flops 1 | bytes 1 | tf_op jit(solution)/shard_map/roll_in/pallas_call | solution.py:438
  56.0 1.8 collective-permute-start.9
  57.7 36.8 %block.4 = (f32[4,432,256]{2,1,0:T(8,128)}, f32[4,432,256]{2,1,0:T(8,128)}, f32[4,144,512]{2,1,0:T(8,128)}, f32[3328,256]{1,0:T(8,128)}, f32[144,1152]{1,0:T(8,128)}, /*index=5*/f32[8,2560]{1,0:T(8,128)}) custom-call(s32[2]{0:T(128)} %bitcast.41, f32[4,432,256]{2,1,0:T(8,128)} %collective-permute-done.6.recv_ref, f32[2,18,192,256]{3,2,1,0:T(8,128)} %bitcast.60, ...), custom_call_target="tpu_custom_call" | custom-call | flops 40000000000 | bytes 1 | tf_op jit(solution)/shard_map/block/pallas_call | solution.py:1068
  94.5 0.3 collective-permute-start.10
  94.9 38.1 %block.5 = (f32[4,432,256]{2,1,0:T(8,128)}, f32[4,432,256]{2,1,0:T(8,128)}, f32[4,144,512]{2,1,0:T(8,128)}, f32[3328,256]{1,0:T(8,128)}, f32[144,1152]{1,0:T(8,128)}, /*index=5*/f32[8,2560]{1,0:T(8,128)}) custom-call(s32[2]{0:T(128)} %bitcast.42, ...), custom_call_target="tpu_custom_call", output_to_operand_aliasing={{3}: (18, {}), {4}: (19, {}), {5}: (20, {})} | custom-call | flops 40000000000 | bytes 1 | tf_op jit(solution)/shard_map/block/pallas_call | solution.py:1068
  133.0 0.5 collective-permute-start.11
  133.6 38.1 %block.6 = (f32[4,432,256]{2,1,0:T(8,128)}, f32[4,432,256]{2,1,0:T(8,128)}, f32[4,144,512]{2,1,0:T(8,128)}, f32[3328,256]{1,0:T(8,128)}, f32[144,1152]{1,0:T(8,128)}, /*index=5*/f32[8,2560]{1,0:T(8,128)}) custom-call(s32[2]{0:T(128)} %bitcast.43, ...), custom_call_target="tpu_custom_call", output_to_operand_aliasing={{3}: (18, {}), {4}: (19, {}), {5}: (20, {})} | custom-call | flops 40000000000 | bytes 1 | tf_op jit(solution)/shard_map/block/pallas_call | solution.py:1068
  171.7 0.6 collective-permute-start.12
  172.3 1.1 copy-done.3
  173.4 4.4 %roll_back.6.refs_3_ = f32[2,18,80,256]{3,2,1,0:T(8,128)} custom-call(s32[2]{0:T(128)S(1)} %bitcast.45, f32[4,432,256]{2,1,0:T(8,128)} %get-tuple-element.78.refs_1_.refs_2_.refs_3_.refs_4_.refs_5_, f32[4,432,256]{2,1,0:T(8,128)} %get-tuple-element.78.refs_1_.refs_2_.refs_3_.refs_4_.refs_5_, ...), custom_call_target="tpu_custom_call" | custom-call | flops 1 | bytes 1 | tf_op jit(solution)/shard_map/roll_back/pallas_call | solution.py:556
  177.7 1.6 collective-permute-start.14
  179.3 38.2 %block.7 = (f32[4,432,256]{2,1,0:T(8,128)}, f32[4,432,256]{2,1,0:T(8,128)}, f32[4,144,512]{2,1,0:T(8,128)}, f32[3328,256]{1,0:T(8,128)}, f32[144,1152]{1,0:T(8,128)}, /*index=5*/f32[8,2560]{1,0:T(8,128)}) custom-call(s32[2]{0:T(128)} %bitcast.44, ...), custom_call_target="tpu_custom_call", output_to_operand_aliasing={{3}: (18, {}), {4}: (19, {}), {5}: (20, {})} | custom-call | flops 40000000000 | bytes 1 | tf_op jit(solution)/shard_map/block/pallas_call | solution.py:1068
  217.6 1.1 copy-done.4
  218.6 2.3 roll_back.7.refs_1_
  220.9 1.5 collective-permute-start.15
  222.5 0.4 collective-permute-start.13
  222.9 3.4 collect.1.in_ref
  226.4 68.9 %scattered_sum.1.refs_9_.refs_0_ = f32[416,256]{1,0:T(8,128)S(1)} custom-call(f32[3328,256]{1,0:T(8,128)S(1)} %collect.1.in_ref), custom_call_target="tpu_custom_call" | custom-call | flops 1 | bytes 1 | tf_op jit(solution)/shard_map/scattered_sum/pallas_call | solution.py:255
  295.2 3.4 collective-permute-start.18
  298.6 2.8 roll_back.8.refs_11_
  301.4 0.6 collective-permute-start.17
  302.0 1.9 roll_back.9.refs_17_
  303.9 1.5 collective-permute-start.16
  305.3 1.5 collective-permute-start.20
  306.8 20.3 %collective-permute-done.18.refs_0_ = f32[416,256]{1,0:T(8,128)S(1)} collective-permute-done((f32[416,256]{1,0:T(8,128)S(1)}, f32[416,256]{1,0:T(8,128)S(1)}, u32[]{:S(2)}, u32[]{:S(2)}) %collective-permute-start.18) | collective-permute-done | bytes 426016 | tf_op jit(solution)/shard_map/ppermute | solution.py:47
  327.1 4.3 %roll_back.10.refs_23_ = f32[2,18,192,256]{3,2,1,0:T(8,128)} custom-call(s32[2]{0:T(128)S(1)} %bitcast.49, f32[4,432,256]{2,1,0:T(8,128)} %get-tuple-element.83.refs_1_.refs_2_.refs_3_.refs_4_.refs_10_.refs_11_, f32[4,432,256]{2,1,0:T(8,128)} %get-tuple-element.83.refs_1_.refs_2_.refs_3_.refs_4_.refs_10_.refs_11_, ...), custom_call_target="tpu_custom_call" | custom-call | flops 1 | bytes 1 | tf_op jit(solution)/shard_map/roll_back/pallas_call | solution.py:556
  331.4 5.3 %roll_back.11.refs_0_ = f32[2,18,192,256]{3,2,1,0:T(8,128)} custom-call(s32[2]{0:T(128)S(1)} %bitcast.50, f32[4,432,256]{2,1,0:T(8,128)} %get-tuple-element.70.refs_5_.refs_6_.refs_7_.refs_8_.refs_1_, f32[4,432,256]{2,1,0:T(8,128)} %get-tuple-element.74.refs_2_.refs_3_.refs_4_.refs_5_, ...), custom_call_target="tpu_custom_call", output_to_operand_aliasing={{}: (23, {})} | custom-call | flops 1 | bytes 1 | tf_op jit(solution)/shard_map/roll_back/pallas_call | solution.py:556
  336.7 3.0 place.4.refs_0_
  339.7 1.6 place.5.refs_0_.refs_3_
  341.5 0.6 collective-permute-start.22
  342.1 0.4 collective-permute-start.24
  342.6 0.1 copy.56
  342.8 0.8 collective-permute-done.22.refs_5_
  343.6 0.6 collective-permute-done.23.refs_6_
  344.2 0.6 collective-permute-done.24.refs_7_
  344.8 4.4 %finish.1 = (f32[256,512]{1,0:T(8,128)}, f32[1,512]{1,0:T(1,128)}, f32[256,768]{1,0:T(8,128)}, f32[8,759]{1,0:T(8,128)}, f32[256,256]{1,0:T(8,128)}, /*index=5*/...) custom-call(s32[2]{0:T(128)S(1)} %pad_add_fusion.place_ref, ...), custom_call_target="tpu_custom_call" | custom-call | flops 1 | bytes 1 | tf_op jit(solution)/shard_map/finish/pallas_call | solution.py:359
  349.2 2.1 place.6.refs_0_
  351.4 3.5 collective-permute-done.16.piece_hbm
  354.8 2.2 place.7
  (75 shorter events, 0.6 us)
Async XLA Ops:
  0.6 29.6 %copy-start = (f32[256,512]{1,0:T(8,128)S(1)}, f32[256,512]{1,0:T(8,128)}, u32[]{:S(2)}) copy-start(f32[256,512]{1,0:T(8,128)} %param.26) | copy-start | bytes 1572868
  1.9 8.3 %collective-permute-start.1 = (f32[2,5,64,256]{3,2,1,0:T(8,128)S(1)}, f32[2,5,64,256]{3,2,1,0:T(8,128)S(1)}, u32[]{:S(2)}, u32[]{:S(2)}) collective-permute-start(f32[2,5,64,256]{3,2,1,0:T(8,128)S(1)} %slice.30), channel_id=1, source_target_pairs={{0,7},{1,0},{2,1},{3,2},{4,3},{5,4},{6,5},{7,6},{8,15},{9,8},{10,9... | collective-permute-start | bytes 1966088 | tf_op jit(solution)/shard_map/ppermute | solution.py:47
  2.7 7.5 %collective-permute-start.3 = (f32[2,5,192]{2,1,0:T(8,128)S(1)}, f32[2,5,192]{2,1,0:T(8,128)S(1)}, u32[]{:S(2)}, u32[]{:S(2)}) collective-permute-start(f32[2,5,192]{2,1,0:T(8,128)S(1)} %slice.32), channel_id=1, source_target_pairs={{0,7},{1,0},{2,1},{3,2},{4,3},{5,4},{6,5},{7,6},{8,15},{9,8},{10,9... | collective-permute-start | bytes 23048 | tf_op jit(solution)/shard_map/ppermute | solution.py:47
  3.3 4.6 %collective-permute-start = (s32[2]{0:T(128)}, s32[2]{0:T(128)S(1)}, u32[]{:S(2)}, u32[]{:S(2)}) collective-permute-start(s32[2]{0:T(128)} %bitcast.40), channel_id=1, source_target_pairs={{0,24},{8,0},{16,8},{24,16},{1,25},{9,1},{17,9},{25,17},{2,26},{10... | collective-permute-start | bytes 32 | tf_op jit(solution)/shard_map/ppermute | solution.py:47
  13.9 43.9 %collective-permute-start.6 = (f32[4,432,256]{2,1,0:T(8,128)}, f32[4,432,256]{2,1,0:T(8,128)}, u32[]{:S(2)}, u32[]{:S(2)}) collective-permute-start(f32[4,432,256]{2,1,0:T(8,128)} %roll_in.4.refs_4_.refs_0_), channel_id=1, source_target_pairs={{0,8},{8,16},{16,24},{24,0},{1,9},{9,17},{17,25},{25,1},{2,10},{10... | collective-permute-start | bytes 5308424 | tf_op jit(solution)/shard_map/ppermute | solution.py:47
  18.0 21.4 %collective-permute-start.2 = (f32[2,5,128,256]{3,2,1,0:T(8,128)}, f32[2,5,128,256]{3,2,1,0:T(8,128)S(1)}, u32[]{:S(2)}, u32[]{:S(2)}) collective-permute-start(f32[2,5,128,256]{3,2,1,0:T(8,128)} %slice.31), channel_id=1, source_target_pairs={{0,7},{1,0},{2,1},{3,2},{4,3},{5,4},{6,5},{7,6},{8,15},{9,8},{10,9... | collective-permute-start | bytes 3932168 | tf_op jit(solution)/shard_map/ppermute | solution.py:47
  19.6 5.6 %copy-start.10 = (s32[1,2]{1,0:T(1,128)S(1)}, s32[1,2]{1,0:T(1,128)}, u32[]{:S(2)}) copy-start(s32[1,2]{1,0:T(1,128)} %param.23) | copy-start | bytes 28
  19.6 11.8 %copy-start.17 = (f32[512]{0:T(512)S(1)}, f32[512]{0:T(512)}, u32[]{:S(2)}) copy-start(f32[512]{0:T(512)} %param.27) | copy-start | bytes 6148
  19.6 11.8 %copy-start.15 = (f32[8,759]{1,0:T(8,128)S(1)}, f32[8,759]{1,0:T(8,128)}, u32[]{:S(2)}) copy-start(f32[8,759]{1,0:T(8,128)} %param.29) | copy-start | bytes 72868
  19.6 12.4 %copy-start.18 = (f32[256]{0:T(256)S(1)}, f32[256]{0:T(256)}, u32[]{:S(2)}) copy-start(f32[256]{0:T(256)} %param.37) | copy-start | bytes 3076
  19.6 12.4 %copy-start.19 = (f32[256]{0:T(256)S(1)}, f32[256]{0:T(256)}, u32[]{:S(2)}) copy-start(f32[256]{0:T(256)} %param.33) | copy-start | bytes 3076
  19.6 12.4 %copy-start.20 = (f32[256]{0:T(256)S(1)}, f32[256]{0:T(256)}, u32[]{:S(2)}) copy-start(f32[256]{0:T(256)} %param.32) | copy-start | bytes 3076
  19.6 12.4 %copy-start.21 = (f32[256]{0:T(256)S(1)}, f32[256]{0:T(256)}, u32[]{:S(2)}) copy-start(f32[256]{0:T(256)} %param.31) | copy-start | bytes 3076
  23.1 2.6 copy-start.14
  23.1 32.8 %collective-permute-start.7 = (f32[2,2,5,64,256]{4,3,2,1,0:T(8,128)}, f32[2,2,5,64,256]{4,3,2,1,0:T(8,128)}, u32[]{:S(2)}, u32[]{:S(2)}) collective-permute-start(f32[2,2,5,64,256]{4,3,2,1,0:T(8,128)} %get-tuple-element.66), channel_id=1, source_target_pairs={{0,7},{1,0},{2,1},{3,2},{4,3},{5,4},{6,5},{7,6},{8,15},{9,8},{10,9... | collective-permute-start | bytes 3932168 | tf_op jit(solution)/shard_map/ppermute | solution.py:47
  35.9 58.9 %collective-permute-start.5 = (f32[2,2,5,160,256]{4,3,2,1,0:T(8,128)}, f32[2,2,5,160,256]{4,3,2,1,0:T(8,128)}, u32[]{:S(2)}, u32[]{:S(2)}) collective-permute-start(f32[2,2,5,160,256]{4,3,2,1,0:T(8,128)} %copy-done.14), channel_id=1, source_target_pairs={{0,7},{1,0},{2,1},{3,2},{4,3},{5,4},{6,5},{7,6},{8,15},{9,8},{10,9... | collective-permute-start | bytes 9830408 | tf_op jit(solution)/shard_map/ppermute | solution.py:47
  43.1 5.8 %copy-start.5 = (bf16[256,1024]{1,0:T(8,128)(2,1)S(1)}, bf16[256,1024]{1,0:T(8,128)(2,1)}, u32[]{:S(2)}) copy-start(bf16[256,1024]{1,0:T(8,128)(2,1)} %w_up_ref.7) | copy-start | bytes 1572868
  43.1 5.8 %copy-start.6 = (bf16[1024,256]{1,0:T(8,128)(2,1)S(1)}, bf16[1024,256]{1,0:T(8,128)(2,1)}, u32[]{:S(2)}) copy-start(bf16[1024,256]{1,0:T(8,128)(2,1)} %w_down_ref.7) | copy-start | bytes 1572868
  43.1 5.8 %copy-start.7 = (bf16[256,768]{1,0:T(8,128)(2,1)S(1)}, bf16[256,768]{1,0:T(8,128)(2,1)}, u32[]{:S(2)}) copy-start(bf16[256,768]{1,0:T(8,128)(2,1)} %w_qkv_ref.7) | copy-start | bytes 1179652
  43.1 5.8 %copy-start.8 = (bf16[256,256]{1,0:T(8,128)(2,1)S(1)}, bf16[256,256]{1,0:T(8,128)(2,1)}, u32[]{:S(2)}) copy-start(bf16[256,256]{1,0:T(8,128)(2,1)} %w_out_ref.7) | copy-start | bytes 393220
  43.1 51.7 %collective-permute-start.4 = (f32[4,432,256]{2,1,0:T(8,128)}, f32[4,432,256]{2,1,0:T(8,128)}, u32[]{:S(2)}, u32[]{:S(2)}) collective-permute-start(f32[4,432,256]{2,1,0:T(8,128)} %roll_in.5.refs_4_.refs_0_.refs_3_), channel_id=1, source_target_pairs={{0,8},{8,16},{16,24},{24,0},{1,9},{9,17},{17,25},{25,1},{2,10},{10... | collective-permute-start | bytes 5308424 | tf_op jit(solution)/shard_map/ppermute | solution.py:47
  48.4 85.2 %collective-permute-start.8 = (f32[4,432,256]{2,1,0:T(8,128)}, f32[4,432,256]{2,1,0:T(8,128)}, u32[]{:S(2)}, u32[]{:S(2)}) collective-permute-start(f32[4,432,256]{2,1,0:T(8,128)} %roll_in.6.refs_4_), channel_id=1, source_target_pairs={{0,8},{8,16},{16,24},{24,0},{1,9},{9,17},{17,25},{25,1},{2,10},{10... | collective-permute-start | bytes 5308424 | tf_op jit(solution)/shard_map/ppermute | solution.py:47
  56.0 123.4 %collective-permute-start.9 = (f32[4,432,256]{2,1,0:T(8,128)}, f32[4,432,256]{2,1,0:T(8,128)}, u32[]{:S(2)}, u32[]{:S(2)}) collective-permute-start(f32[4,432,256]{2,1,0:T(8,128)} %roll_in.7), channel_id=1, source_target_pairs={{0,8},{8,16},{16,24},{24,0},{1,9},{9,17},{17,25},{25,1},{2,10},{10... | collective-permute-start | bytes 5308424 | tf_op jit(solution)/shard_map/ppermute | solution.py:47
  94.5 77.7 %collective-permute-start.10 = (f32[4,144,512]{2,1,0:T(8,128)}, f32[4,144,512]{2,1,0:T(8,128)S(1)}, u32[]{:S(2)}, u32[]{:S(2)}) collective-permute-start(f32[4,144,512]{2,1,0:T(8,128)} %get-tuple-element.80), channel_id=1, source_target_pairs={{0,1},{1,2},{2,3},{3,4},{4,5},{5,6},{6,7},{7,0},{8,9},{9,10},{10,1... | collective-permute-start | bytes 3538952 | tf_op jit(solution)/shard_map/ppermute | solution.py:47
  133.0 39.3 %collective-permute-start.11 = (f32[4,144,512]{2,1,0:T(8,128)}, f32[4,144,512]{2,1,0:T(8,128)}, u32[]{:S(2)}, u32[]{:S(2)}) collective-permute-start(f32[4,144,512]{2,1,0:T(8,128)} %get-tuple-element.81), channel_id=1, source_target_pairs={{0,1},{1,2},{2,3},{3,4},{4,5},{5,6},{6,7},{7,0},{8,9},{9,10},{10,1... | collective-permute-start | bytes 3538952 | tf_op jit(solution)/shard_map/ppermute | solution.py:47
  133.5 38.7 %copy-start.11 = (s32[1,2]{1,0:T(1,128)S(1)}, s32[1,2]{1,0:T(1,128)}, u32[]{:S(2)}) copy-start(s32[1,2]{1,0:T(1,128)} %param.23) | copy-start | bytes 28
  171.7 45.8 %collective-permute-start.12 = (f32[4,144,512]{2,1,0:T(8,128)}, f32[4,144,512]{2,1,0:T(8,128)}, u32[]{:S(2)}, u32[]{:S(2)}) collective-permute-start(f32[4,144,512]{2,1,0:T(8,128)} %get-tuple-element.84), channel_id=1, source_target_pairs={{0,1},{1,2},{2,3},{3,4},{4,5},{5,6},{6,7},{7,0},{8,9},{9,10},{10,1... | collective-permute-start | bytes 3538952 | tf_op jit(solution)/shard_map/ppermute | solution.py:47
  172.3 1.1 copy-start.3
  177.7 120.9 %collective-permute-start.14 = (f32[2,18,80,256]{3,2,1,0:T(8,128)}, f32[2,18,80,256]{3,2,1,0:T(8,128)}, u32[]{:S(2)}, u32[]{:S(2)}) collective-permute-start(f32[2,18,80,256]{3,2,1,0:T(8,128)} %roll_back.6.refs_3_), channel_id=1, source_target_pairs={{0,24},{8,0},{16,8},{24,16},{1,25},{9,1},{17,9},{25,17},{2,26},{10... | collective-permute-start | bytes 8847368 | tf_op jit(solution)/shard_map/ppermute | solution.py:47
  179.3 38.2 %copy-start.12 = (s32[1,2]{1,0:T(1,128)S(1)}, s32[1,2]{1,0:T(1,128)}, u32[]{:S(2)}) copy-start(s32[1,2]{1,0:T(1,128)} %param.23) | copy-start | bytes 28
  217.5 1.1 copy-start.4
  218.6 3.8 %copy-start.22 = (f32[4,144,512]{2,1,0:T(8,128)S(1)}, f32[4,144,512]{2,1,0:T(8,128)}, u32[]{:S(2)}) copy-start(f32[4,144,512]{2,1,0:T(8,128)} %get-tuple-element.85) | copy-start | bytes 3538948
  218.6 4.3 %copy-start.2 = (f32[3328,256]{1,0:T(8,128)S(1)}, f32[3328,256]{1,0:T(8,128)}, u32[]{:S(2)}) copy-start(f32[3328,256]{1,0:T(8,128)} %get-tuple-element.90.refs_0_) | copy-start | bytes 10223620
  218.6 4.3 %copy-start.9 = (f32[8,2560]{1,0:T(8,128)S(1)}, f32[8,2560]{1,0:T(8,128)}, u32[]{:S(2)}) copy-start(f32[8,2560]{1,0:T(8,128)} %get-tuple-element.89.small_ref) | copy-start | bytes 245764
  220.9 77.7 %collective-permute-start.15 = (f32[2,18,48,256]{3,2,1,0:T(8,128)S(1)}, f32[2,18,48,256]{3,2,1,0:T(8,128)S(1)}, u32[]{:S(2)}, u32[]{:S(2)}) collective-permute-start(f32[2,18,48,256]{3,2,1,0:T(8,128)S(1)} %roll_back.7.refs_1_), channel_id=1, source_target_pairs={{0,24},{8,0},{16,8},{24,16},{1,25},{9,1},{17,9},{25,17},{2,26},{10... | collective-permute-start | bytes 5308424 | tf_op jit(solution)/shard_map/ppermute | solution.py:47
  222.5 76.1 %collective-permute-start.13 = (f32[4,144,512]{2,1,0:T(8,128)S(1)}, f32[4,144,512]{2,1,0:T(8,128)S(1)}, u32[]{:S(2)}, u32[]{:S(2)}) collective-permute-start(f32[4,144,512]{2,1,0:T(8,128)S(1)} %copy-done.22), channel_id=1, source_target_pairs={{0,1},{1,2},{2,3},{3,4},{4,5},{5,6},{6,7},{7,0},{8,9},{9,10},{10,1... | collective-permute-start | bytes 3538952 | tf_op jit(solution)/shard_map/ppermute | solution.py:47
  295.2 31.9 %collective-permute-start.18 = (f32[416,256]{1,0:T(8,128)S(1)}, f32[416,256]{1,0:T(8,128)S(1)}, u32[]{:S(2)}, u32[]{:S(2)}) collective-permute-start(f32[416,256]{1,0:T(8,128)S(1)} %scattered_sum.1.refs_9_.refs_0_), channel_id=1, source_target_pairs={{0,2},{1,3},{2,4},{3,5},{4,6},{5,7},{6,0},{7,1},{8,10},{9,11},{10,... | collective-permute-start | bytes 1277960 | tf_op jit(solution)/shard_map/ppermute | solution.py:47
  301.4 25.7 %copy-start.13 = (s32[1,2]{1,0:T(1,128)S(1)}, s32[1,2]{1,0:T(1,128)}, u32[]{:S(2)}) copy-start(s32[1,2]{1,0:T(1,128)} %param.23) | copy-start | bytes 28
  301.4 47.8 %collective-permute-start.17 = (f32[2,18,32,256]{3,2,1,0:T(8,128)}, f32[2,18,32,256]{3,2,1,0:T(8,128)}, u32[]{:S(2)}, u32[]{:S(2)}) collective-permute-start(f32[2,18,32,256]{3,2,1,0:T(8,128)} %roll_back.8.refs_11_), channel_id=1, source_target_pairs={{0,24},{8,0},{16,8},{24,16},{1,25},{9,1},{17,9},{25,17},{2,26},{10... | collective-permute-start | bytes 3538952 | tf_op jit(solution)/shard_map/ppermute | solution.py:47
  303.9 51.0 %collective-permute-start.16 = (f32[2,18,32,256]{3,2,1,0:T(8,128)S(1)}, f32[2,18,32,256]{3,2,1,0:T(8,128)}, u32[]{:S(2)}, u32[]{:S(2)}) collective-permute-start(f32[2,18,32,256]{3,2,1,0:T(8,128)S(1)} %roll_back.9.refs_17_), channel_id=1, source_target_pairs={{0,24},{8,0},{16,8},{24,16},{1,25},{9,1},{17,9},{25,17},{2,26},{10... | collective-permute-start | bytes 3538952 | tf_op jit(solution)/shard_map/ppermute | solution.py:47
  305.3 36.0 %collective-permute-start.19 = (f32[416,256]{1,0:T(8,128)S(1)}, f32[416,256]{1,0:T(8,128)S(1)}, u32[]{:S(2)}, u32[]{:S(2)}) collective-permute-start(f32[416,256]{1,0:T(8,128)S(1)} %scattered_sum.1.refs_9_.refs_0_), channel_id=1, source_target_pairs={{0,4},{1,5},{2,6},{3,7},{4,0},{5,1},{6,2},{7,3},{8,12},{9,13},{10,... | collective-permute-start | bytes 1277960 | tf_op jit(solution)/shard_map/ppermute | solution.py:47
  305.3 36.0 %collective-permute-start.20 = (f32[416,256]{1,0:T(8,128)S(1)}, f32[416,256]{1,0:T(8,128)S(1)}, u32[]{:S(2)}, u32[]{:S(2)}) collective-permute-start(f32[416,256]{1,0:T(8,128)S(1)} %scattered_sum.1.refs_9_.refs_0_), channel_id=1, source_target_pairs={{0,6},{1,7},{2,0},{3,1},{4,2},{5,3},{6,4},{7,5},{8,14},{9,15},{10,... | collective-permute-start | bytes 1277960 | tf_op jit(solution)/shard_map/ppermute | solution.py:47
  327.1 15.0 %collective-permute-start.21 = (f32[416,256]{1,0:T(8,128)S(1)}, f32[416,256]{1,0:T(8,128)S(1)}, u32[]{:S(2)}, u32[]{:S(2)}) collective-permute-start(f32[416,256]{1,0:T(8,128)S(1)} %scattered_sum.1.refs_9_.refs_0_), channel_id=1, source_target_pairs={{0,1},{1,0},{2,3},{3,2},{4,5},{5,4},{6,7},{7,6},{8,9},{9,8},{10,11... | collective-permute-start | bytes 1277960 | tf_op jit(solution)/shard_map/ppermute | solution.py:299
  341.4 1.2 copy-start.16
  341.5 2.1 collective-permute-start.22
  342.1 2.1 collective-permute-start.23
  342.1 2.7 collective-permute-start.24
  354.8 2.2 copy-start.1
